TPU v7x, 128 devices: a whole 4x4x4 slice. The times are simulated.
128 devices in a mesh: atm: 32 (over x, y, core), ocn: 4 (over z).
Axes of the slice: x: 4, y: 4, z: 4, core: 2. Of those that a mesh axis runs over, the one named last changes fastest.
Arguments:
- source_flux: bfloat16 [4, 262144], P(None, ('atm', 'ocn')), may hold values from -6 to 6
- remap_weights: bfloat16 [73728, 128, 128], P(('atm', 'ocn')), may hold values from -0.1875 to 0.1875
- source_block: int32 [73728], P(('atm', 'ocn')), may hold values from 0 to 15
- owner_device: int32 [73728, 1], P(('atm', 'ocn')), may hold values from 0 to 127; in each aligned block of 576 rows (0 to 575, 576 to 1151, ...) at most 9 rows name the same one
- target_row: int32 [73728], P(('atm', 'ocn')), may hold values from 0 to 63
- sea_height: float32 [2048, 512], P('atm', 'ocn'), may hold values from -6 to 6
- u_velocity: float32 [2048, 512], P('atm', 'ocn'), may hold values from -6 to 6
- v_velocity: float32 [2048, 512], P('atm', 'ocn'), may hold values from -6 to 6
- ocean_depth: float32 [2048, 512], P('atm', 'ocn'), may hold values from 0.5 to 2
Outputs:
- ocean_flux: float32 [4, 2048, 512], P(None, 'atm', 'ocn')
- height_next: float32 [2048, 512], P('atm', 'ocn')
- zonal_next: float32 [2048, 512], P('atm', 'ocn')
- merid_next: float32 [2048, 512], P('atm', 'ocn')
Inputs may be any that keep to these rules, and one draw needn't show every extreme that they name: `owner_device`: among the 576 weight blocks of one device no owner is named more than 9 times, a bound that some block reaches.
All inputs are finite; a program needn't handle non-finite values.
Results may differ from a plain program's by a relative error of at most 0.0003.
Values sent between devices are 32-bit elements; how exact they have to be, the bound alone decides.
No kernel may reach another device: no remote copies, remote signals or barrier semaphores. Data moves between devices by JAX's collectives and lax.ppermute only.
A program may use at most 64 MiB of HBM per device.

v0:
```python
import jax
import jax.numpy as jnp
from jax import lax
from jax.sharding import PartitionSpec as P

CX = 64
STEPS = 3


courant = 0.5
forcing = 0.3
coriolis = 0.2
damping = 0.05
steric = 0.5


def padded_2(x, sides, width):
    for axis, dim in sides:
        devices, length = (lax.axis_size(axis), x.shape[dim])
        up = [(i, (i + 1) % devices) for i in range(devices - 1)]
        down = [(j, i) for i, j in up]
        last = lax.slice_in_dim(x, length - width, length, axis=dim)
        initial = lax.slice_in_dim(x, 0, width, axis=dim)
        before = lax.ppermute(last, axis, up)
        after = lax.ppermute(initial, axis, down)
        x = jnp.concatenate([before, x, after], axis=dim)
    return x


def grad_x(padded):
    return 0.5 * (padded[2:, 1:-1] - padded[:-2, 1:-1])


def grad_y(padded):
    return 0.5 * (padded[1:-1, 2:] - padded[1:-1, :-2])


def on_device(
    source_flux,
    remap_weights,
    source_block,
    owner_device,
    target_row,
    sea_height,
    u_velocity,
    v_velocity,
    ocean_depth,
):
    fields = source_flux.shape[0]
    block_width = remap_weights.shape[1]
    count = remap_weights.shape[0]
    atm_count = lax.axis_size("atm")
    ocn_count = lax.axis_size("ocn")
    devices = atm_count * ocn_count
    capacity = max(2, (2 * count + devices - 1) // devices)
    blocks = source_flux.reshape(fields, -1, block_width)
    picked = jnp.take(blocks, source_block, axis=1)
    contrib = jnp.einsum("fwb,wbc->wfc", picked, remap_weights, preferred_element_type=jnp.float32)
    owner_ids = owner_device[:, 0]
    matches = owner_ids[:, None] == owner_ids[None, :]
    positions = jnp.arange(count)
    earlier = positions[None, :] < positions[:, None]
    slot_rank = jnp.sum((matches & earlier).astype(jnp.int32), axis=1)
    slot_ids = owner_ids * capacity + slot_rank
    buffer = (
        jnp.zeros((devices * capacity, fields, block_width), jnp.float32).at[slot_ids].set(contrib)
    )
    labels = (
        jnp.full((devices * capacity,), -1.0, jnp.float32)
        .at[slot_ids]
        .set(target_row.astype(jnp.float32))
    )
    arrived, arrived_rows = (
        lax.all_to_all(buffer, ("atm", "ocn"), split_axis=0, concat_axis=0, tiled=True),
        lax.all_to_all(labels, ("atm", "ocn"), split_axis=0, concat_axis=0, tiled=True),
    )
    onehot = (arrived_rows[None, :] == jnp.arange(CX, dtype=jnp.float32)[:, None]).astype(
        jnp.float32
    )
    flux_local = jnp.einsum("rs,sfc->frc", onehot, arrived, precision=lax.Precision.HIGHEST)
    source = forcing * (flux_local[2] + steric * flux_local[3])
    height = sea_height
    zonal_flow = u_velocity
    merid_flow = v_velocity
    for substep in range(STEPS):
        zonal_pad, merid_pad = (
            padded_2(zonal_flow, (("atm", 0), ("ocn", 1)), 1),
            padded_2(merid_flow, (("atm", 0), ("ocn", 1)), 1),
        )
        height = height - courant * ocean_depth * (grad_x(zonal_pad) + grad_y(merid_pad)) + source
        height_pad = padded_2(height, (("atm", 0), ("ocn", 1)), 1)
        new_zonal = (
            zonal_flow
            - courant * grad_x(height_pad)
            + coriolis * merid_flow
            + forcing * flux_local[0]
            - damping * zonal_flow
        )
        new_merid = (
            merid_flow
            - courant * grad_y(height_pad)
            - coriolis * zonal_flow
            + forcing * flux_local[1]
            - damping * merid_flow
        )
        zonal_flow = new_zonal
        merid_flow = new_merid
    return (flux_local, height, zonal_flow, merid_flow)


def solution(mesh):
    placed = (
        P(None, ("atm", "ocn")),
        P(("atm", "ocn"), None, None),
        P(("atm", "ocn")),
        P(("atm", "ocn"), None),
        P(("atm", "ocn")),
        P("atm", "ocn"),
        P("atm", "ocn"),
        P("atm", "ocn"),
        P("atm", "ocn"),
    )
    return jax.shard_map(
        on_device,
        mesh=mesh,
        in_specs=placed,
        out_specs=(P(None, "atm", "ocn"), P("atm", "ocn"), P("atm", "ocn"), P("atm", "ocn")),
        check_vma=False,
    )
```

profile of v0, /device:TPU:4, one launch (start us, length us, event | category | flops | bytes accessed | tf_op | source)
XLA Modules:
  0.0 229.8 jit_solution(13921574154179571944)
XLA Ops:
  0.6 0.7 reduce
  1.3 0.3 convert_reduce_fusion
  1.6 0.7 fusion.78
  2.3 0.7 convert_element_type.8
  3.0 4.1 %scatter_custom_fusion.1 = f32[1152]{0:T(1024)S(1)} fusion(s32[576]{0:T(1024)S(1)} %fusion.78, f32[576]{0:T(1024)S(1)} %convert_element_type.8, f32[]{:T(128)} %constant.35.clone.1), kind=kCustom, calls=%fused_computation.139 | custom fusion | bytes 4612 | tf_op jit(solution)/shard_map/scatter | solution.py:71
  7.1 0.8 all_to_all.10
  8.0 10.5 %all-to-all-start.1 = ((f32[128,9,1]{1,2,0:T(1,128)}), f32[128,9,1]{1,2,0:T(1,128)S(1)}, u32[]{:S(2)}, u32[]{:S(2)}) async-start(f32[128,9,1]{1,2,0:T(1,128)} %bitcast.2), calls=%async_computation.1 | async-start | bytes 131072 | tf_op jit(solution)/shard_map/all_to_all | solution.py:75
  18.5 0.7 compare_select_fusion.1
  19.2 0.7 compare_and_fusion
  19.9 2.8 %gather_fusion = bf16[576,4,128]{2,1,0:T(4,128)(2,1)S(1)} fusion(bf16[4,16,128]{2,0,1:T(4,128)(2,1)S(1)} %bitcast.36, s32[1024]{0:T(1024)S(1)} %pad_clamp_fusion), kind=kCustom, calls=%fused_computation | custom fusion | bytes 1181952 | tf_op jit(solution)/shard_map/jit(_take)/gather | solution.py:57
  22.6 9.0 %fusion.6 = f32[576,4,128]{2,1,0:T(4,128)S(1)} fusion(bf16[576,128,128]{2,1,0:T(8,128)(2,1)} %param.10, bf16[576,4,128]{2,1,0:T(4,128)(2,1)S(1)} %gather_fusion, pred[576]{0:T(1024)(128)(4,1)S(1)} %compare_and_fusion), kind=kOutput, calls=%fused_computation.9 | convolution fusion | flops 75792384 | bytes 20644416 | tf_op jit(solution)/shard_map/fwb,wbc->wfc/dot_general | solution.py:58
  31.6 1.6 broadcast_in_dim.24
  33.2 54.7 %scatter_fusion = f32[1152,4,128]{2,1,0:T(4,128)} fusion(f32[1152,4,128]{2,1,0:T(4,128)} %broadcast_in_dim.24, s32[576]{0:T(1024)S(1)} %fusion.78, f32[576,4,128]{2,1,0:T(4,128)S(1)} %fusion.6), kind=kCustom, calls=%fused_computation.1 | custom fusion | bytes 3541248 | tf_op jit(solution)/shard_map/scatter | solution.py:66
  87.9 9.8 %all-to-all-start = ((f32[1152,4,128]{2,1,0:T(4,128)}), f32[1152,4,128]{2,1,0:T(4,128)S(1)}, u32[]{:S(2)}, u32[]{:S(2)}) async-start(f32[1152,4,128]{2,1,0:T(4,128)} %scatter_fusion), calls=%async_computation | async-start | bytes 4718592 | tf_op jit(solution)/shard_map/all_to_all | solution.py:74
  97.8 2.1 collective-permute-start.2
  99.8 5.6 %collective-permute-start.3 = (f32[1,128]{1,0:T(1,128)S(1)}, f32[1,128]{1,0:T(1,128)S(1)}, u32[]{:S(2)}, u32[]{:S(2)}) collective-permute-start(f32[1,128]{1,0:T(1,128)S(1)} %get-tuple-element.39), channel_id=1, source_target_pairs={{4,0},{8,4},{12,8},{16,12},{20,16},{24,20},{28,24},{32,28},{36,32}... | collective-permute-start | bytes 1544 | tf_op jit(solution)/shard_map/ppermute | solution.py:25
  105.5 1.9 collective-permute-start
  107.4 2.4 %collective-permute-start.1 = (f32[1,128]{1,0:T(1,128)S(1)}, f32[1,128]{1,0:T(1,128)S(1)}, u32[]{:S(2)}, u32[]{:S(2)}) collective-permute-start(f32[1,128]{1,0:T(1,128)S(1)} %get-tuple-element.37), channel_id=1, source_target_pairs={{0,4},{4,8},{8,12},{12,16},{16,20},{20,24},{24,28},{28,32},{32,36}... | collective-permute-start | bytes 1544 | tf_op jit(solution)/shard_map/ppermute | solution.py:24
  109.8 15.9 %collective-permute-done.2 = f32[1,128]{1,0:T(1,128)S(1)} collective-permute-done((f32[1,128]{1,0:T(1,128)S(1)}, f32[1,128]{1,0:T(1,128)S(1)}, u32[]{:S(2)}, u32[]{:S(2)}) %collective-permute-start.2) | collective-permute-done | bytes 544 | tf_op jit(solution)/shard_map/ppermute | solution.py:24
  125.7 0.1 fusion.85
  125.8 1.3 collective-permute-start.4
  127.1 4.5 %collective-permute-start.5 = (f32[66,1]{1,0:T(8,128)S(1)}, f32[66,1]{1,0:T(8,128)S(1)}, u32[]{:S(2)}, u32[]{:S(2)}) collective-permute-start(f32[66,1]{1,0:T(8,128)S(1)} %get-tuple-element.21), channel_id=1, source_target_pairs={{0,1},{1,2},{2,3},{4,5},{5,6},{6,7},{8,9},{9,10},{10,11},{12,13},{... | collective-permute-start | bytes 800 | tf_op jit(solution)/shard_map/ppermute | solution.py:24
  131.6 0.5 broadcast.110
  132.1 0.8 reduce.6
  133.0 0.2 eq.34
  133.2 1.0 fusion.3
  134.3 0.1 fusion.74
  134.4 1.9 collective-permute-start.6
  136.3 2.4 %collective-permute-start.7 = (f32[1,128]{1,0:T(1,128)S(1)}, f32[1,128]{1,0:T(1,128)S(1)}, u32[]{:S(2)}, u32[]{:S(2)}) collective-permute-start(f32[1,128]{1,0:T(1,128)S(1)} %get-tuple-element.34), channel_id=1, source_target_pairs={{0,4},{4,8},{8,12},{12,16},{16,20},{20,24},{24,28},{28,32},{32,36}... | collective-permute-start | bytes 1544 | tf_op jit(solution)/shard_map/ppermute | solution.py:24
  138.8 4.5 %collective-permute-done.7 = f32[1,128]{1,0:T(1,128)S(1)} collective-permute-done((f32[1,128]{1,0:T(1,128)S(1)}, f32[1,128]{1,0:T(1,128)S(1)}, u32[]{:S(2)}, u32[]{:S(2)}) %collective-permute-start.7) | collective-permute-done | bytes 544 | tf_op jit(solution)/shard_map/ppermute | solution.py:24
  143.4 1.3 collective-permute-start.10
  144.7 4.5 %collective-permute-start.11 = (f32[66,1]{1,0:T(8,128)S(1)}, f32[66,1]{1,0:T(8,128)S(1)}, u32[]{:S(2)}, u32[]{:S(2)}) collective-permute-start(f32[66,1]{1,0:T(8,128)S(1)} %get-tuple-element.19), channel_id=1, source_target_pairs={{0,1},{1,2},{2,3},{4,5},{5,6},{6,7},{8,9},{9,10},{10,11},{12,13},{... | collective-permute-start | bytes 800 | tf_op jit(solution)/shard_map/ppermute | solution.py:24
  149.2 1.6 collective-permute-done.11
  150.9 0.1 fusion.65
  151.0 1.9 collective-permute-start.12
  152.9 5.8 %collective-permute-start.13 = (f32[1,128]{1,0:T(1,128)S(1)}, f32[1,128]{1,0:T(1,128)S(1)}, u32[]{:S(2)}, u32[]{:S(2)}) collective-permute-start(f32[1,128]{1,0:T(1,128)S(1)} %get-tuple-element.33), channel_id=1, source_target_pairs={{4,0},{8,4},{12,8},{16,12},{20,16},{24,20},{28,24},{32,28},{36,32}... | collective-permute-start | bytes 1544 | tf_op jit(solution)/shard_map/ppermute | solution.py:25
  158.7 1.9 collective-permute-start.8
  160.6 2.4 %collective-permute-start.9 = (f32[1,128]{1,0:T(1,128)S(1)}, f32[1,128]{1,0:T(1,128)S(1)}, u32[]{:S(2)}, u32[]{:S(2)}) collective-permute-start(f32[1,128]{1,0:T(1,128)S(1)} %get-tuple-element.31), channel_id=1, source_target_pairs={{0,4},{4,8},{8,12},{12,16},{16,20},{20,24},{24,28},{28,32},{32,36}... | collective-permute-start | bytes 1544 | tf_op jit(solution)/shard_map/ppermute | solution.py:24
  163.1 1.3 collective-permute-start.14
  164.4 4.9 %collective-permute-start.15 = (f32[66,1]{1,0:T(8,128)S(1)}, f32[66,1]{1,0:T(8,128)S(1)}, u32[]{:S(2)}, u32[]{:S(2)}) collective-permute-start(f32[66,1]{1,0:T(8,128)S(1)} %get-tuple-element.17), channel_id=1, source_target_pairs={{0,1},{1,2},{2,3},{4,5},{5,6},{6,7},{8,9},{9,10},{10,11},{12,13},{... | collective-permute-start | bytes 800 | tf_op jit(solution)/shard_map/ppermute | solution.py:24
  169.3 1.6 collective-permute-done.15
  170.9 0.1 fusion.50
  171.0 4.4 %collective-permute-start.16 = (f32[1,128]{1,0:T(1,128)S(1)}, f32[1,128]{1,0:T(1,128)S(1)}, u32[]{:S(2)}, u32[]{:S(2)}) collective-permute-start(f32[1,128]{1,0:T(1,128)S(1)} %get-tuple-element.29), channel_id=1, source_target_pairs={{4,0},{8,4},{12,8},{16,12},{20,16},{24,20},{28,24},{32,28},{36,32}... | collective-permute-start | bytes 1544 | tf_op jit(solution)/shard_map/ppermute | solution.py:25
  175.4 1.9 collective-permute-start.17
  177.4 5.0 %collective-permute-done.17 = f32[1,128]{1,0:T(1,128)S(1)} collective-permute-done((f32[1,128]{1,0:T(1,128)S(1)}, f32[1,128]{1,0:T(1,128)S(1)}, u32[]{:S(2)}, u32[]{:S(2)}) %collective-permute-start.17) | collective-permute-done | bytes 544 | tf_op jit(solution)/shard_map/ppermute | solution.py:24
  182.5 1.3 collective-permute-start.20
  183.8 4.6 %collective-permute-start.21 = (f32[66,1]{1,0:T(8,128)S(1)}, f32[66,1]{1,0:T(8,128)S(1)}, u32[]{:S(2)}, u32[]{:S(2)}) collective-permute-start(f32[66,1]{1,0:T(8,128)S(1)} %get-tuple-element.15), channel_id=1, source_target_pairs={{0,1},{1,2},{2,3},{4,5},{5,6},{6,7},{8,9},{9,10},{10,11},{12,13},{... | collective-permute-start | bytes 800 | tf_op jit(solution)/shard_map/ppermute | solution.py:24
  188.4 1.6 collective-permute-done.21
  190.0 0.1 fusion.44
  190.1 1.9 collective-permute-start.22
  192.0 5.8 %collective-permute-start.23 = (f32[1,128]{1,0:T(1,128)S(1)}, f32[1,128]{1,0:T(1,128)S(1)}, u32[]{:S(2)}, u32[]{:S(2)}) collective-permute-start(f32[1,128]{1,0:T(1,128)S(1)} %get-tuple-element.27), channel_id=1, source_target_pairs={{4,0},{8,4},{12,8},{16,12},{20,16},{24,20},{28,24},{32,28},{36,32}... | collective-permute-start | bytes 1544 | tf_op jit(solution)/shard_map/ppermute | solution.py:25
  197.8 1.9 collective-permute-start.18
  199.7 2.4 %collective-permute-start.19 = (f32[1,128]{1,0:T(1,128)S(1)}, f32[1,128]{1,0:T(1,128)S(1)}, u32[]{:S(2)}, u32[]{:S(2)}) collective-permute-start(f32[1,128]{1,0:T(1,128)S(1)} %get-tuple-element.25), channel_id=1, source_target_pairs={{0,4},{4,8},{8,12},{12,16},{16,20},{20,24},{24,28},{28,32},{32,36}... | collective-permute-start | bytes 1544 | tf_op jit(solution)/shard_map/ppermute | solution.py:24
  202.2 1.3 collective-permute-start.24
  203.5 4.9 %collective-permute-start.25 = (f32[66,1]{1,0:T(8,128)S(1)}, f32[66,1]{1,0:T(8,128)S(1)}, u32[]{:S(2)}, u32[]{:S(2)}) collective-permute-start(f32[66,1]{1,0:T(8,128)S(1)} %get-tuple-element.13), channel_id=1, source_target_pairs={{0,1},{1,2},{2,3},{4,5},{5,6},{6,7},{8,9},{9,10},{10,11},{12,13},{... | collective-permute-start | bytes 800 | tf_op jit(solution)/shard_map/ppermute | solution.py:24
  208.4 1.6 collective-permute-done.25
  210.0 0.1 fusion.31
  210.2 4.4 %collective-permute-start.26 = (f32[1,128]{1,0:T(1,128)S(1)}, f32[1,128]{1,0:T(1,128)S(1)}, u32[]{:S(2)}, u32[]{:S(2)}) collective-permute-start(f32[1,128]{1,0:T(1,128)S(1)} %get-tuple-element.22), channel_id=1, source_target_pairs={{4,0},{8,4},{12,8},{16,12},{20,16},{24,20},{28,24},{32,28},{36,32}... | collective-permute-start | bytes 1544 | tf_op jit(solution)/shard_map/ppermute | solution.py:25
  214.6 1.9 collective-permute-start.27
  216.5 5.0 %collective-permute-done.27 = f32[1,128]{1,0:T(1,128)S(1)} collective-permute-done((f32[1,128]{1,0:T(1,128)S(1)}, f32[1,128]{1,0:T(1,128)S(1)}, u32[]{:S(2)}, u32[]{:S(2)}) %collective-permute-start.27) | collective-permute-done | bytes 544 | tf_op jit(solution)/shard_map/ppermute | solution.py:24
  221.6 1.3 collective-permute-start.28
  222.9 4.6 %collective-permute-start.29 = (f32[66,1]{1,0:T(8,128)S(1)}, f32[66,1]{1,0:T(8,128)S(1)}, u32[]{:S(2)}, u32[]{:S(2)}) collective-permute-start(f32[66,1]{1,0:T(8,128)S(1)} %get-tuple-element.11), channel_id=1, source_target_pairs={{0,1},{1,2},{2,3},{4,5},{5,6},{6,7},{8,9},{9,10},{10,11},{12,13},{... | collective-permute-start | bytes 800 | tf_op jit(solution)/shard_map/ppermute | solution.py:24
  227.5 1.6 collective-permute-done.29
  229.1 0.7 fusion.19
  (58 shorter events, 0.6 us)
Async XLA Ops:
  0.6 19.2 %copy-start = (bf16[4,2048]{1,0:T(4,128)(2,1)S(1)}, bf16[4,2048]{1,0:T(4,128)(2,1)}, u32[]{:S(2)}) copy-start(bf16[4,2048]{1,0:T(4,128)(2,1)} %param.9) | copy-start | bytes 49156
  8.0 80.0 %all-to-all-start.1 = ((f32[128,9,1]{1,2,0:T(1,128)}), f32[128,9,1]{1,2,0:T(1,128)S(1)}, u32[]{:S(2)}, u32[]{:S(2)}) async-start(f32[128,9,1]{1,2,0:T(1,128)} %bitcast.2), calls=%async_computation.1 | async-start | bytes 131072 | tf_op jit(solution)/shard_map/all_to_all | solution.py:75
  87.9 9.8 %copy-start.2 = (f32[64,128]{1,0:T(8,128)S(1)}, f32[64,128]{1,0:T(8,128)}, u32[]{:S(2)}) copy-start(f32[64,128]{1,0:T(8,128)} %param.16) | copy-start | bytes 98308
  87.9 17.5 %copy-start.5 = (f32[64,128]{1,0:T(8,128)S(1)}, f32[64,128]{1,0:T(8,128)}, u32[]{:S(2)}) copy-start(f32[64,128]{1,0:T(8,128)} %param.15) | copy-start | bytes 98308
  87.9 45.2 %all-to-all-start = ((f32[1152,4,128]{2,1,0:T(4,128)}), f32[1152,4,128]{2,1,0:T(4,128)S(1)}, u32[]{:S(2)}, u32[]{:S(2)}) async-start(f32[1152,4,128]{2,1,0:T(4,128)} %scatter_fusion), calls=%async_computation | async-start | bytes 4718592 | tf_op jit(solution)/shard_map/all_to_all | solution.py:74
  97.7 36.5 %copy-start.4 = (f32[64,128]{1,0:T(8,128)S(1)}, f32[64,128]{1,0:T(8,128)}, u32[]{:S(2)}) copy-start(f32[64,128]{1,0:T(8,128)} %param.17) | copy-start | bytes 98308
  97.7 36.5 %copy-start.6 = (f32[64,128]{1,0:T(8,128)S(1)}, f32[64,128]{1,0:T(8,128)}, u32[]{:S(2)}) copy-start(f32[64,128]{1,0:T(8,128)} %param.14) | copy-start | bytes 98308
  97.8 27.9 %collective-permute-start.2 = (f32[1,128]{1,0:T(1,128)S(1)}, f32[1,128]{1,0:T(1,128)S(1)}, u32[]{:S(2)}, u32[]{:S(2)}) collective-permute-start(f32[1,128]{1,0:T(1,128)S(1)} %get-tuple-element.38), channel_id=1, source_target_pairs={{0,4},{4,8},{8,12},{12,16},{16,20},{20,24},{24,28},{28,32},{32,36}... | collective-permute-start | bytes 1544 | tf_op jit(solution)/shard_map/ppermute | solution.py:24
  99.8 25.9 %collective-permute-start.3 = (f32[1,128]{1,0:T(1,128)S(1)}, f32[1,128]{1,0:T(1,128)S(1)}, u32[]{:S(2)}, u32[]{:S(2)}) collective-permute-start(f32[1,128]{1,0:T(1,128)S(1)} %get-tuple-element.39), channel_id=1, source_target_pairs={{4,0},{8,4},{12,8},{16,12},{20,16},{24,20},{28,24},{32,28},{36,32}... | collective-permute-start | bytes 1544 | tf_op jit(solution)/shard_map/ppermute | solution.py:25
  105.5 28.8 %collective-permute-start = (f32[1,128]{1,0:T(1,128)S(1)}, f32[1,128]{1,0:T(1,128)S(1)}, u32[]{:S(2)}, u32[]{:S(2)}) collective-permute-start(f32[1,128]{1,0:T(1,128)S(1)} %get-tuple-element.36), channel_id=1, source_target_pairs={{4,0},{8,4},{12,8},{16,12},{20,16},{24,20},{28,24},{32,28},{36,32}... | collective-permute-start | bytes 1544 | tf_op jit(solution)/shard_map/ppermute | solution.py:25
  107.4 26.8 %collective-permute-start.1 = (f32[1,128]{1,0:T(1,128)S(1)}, f32[1,128]{1,0:T(1,128)S(1)}, u32[]{:S(2)}, u32[]{:S(2)}) collective-permute-start(f32[1,128]{1,0:T(1,128)S(1)} %get-tuple-element.37), channel_id=1, source_target_pairs={{0,4},{4,8},{8,12},{12,16},{16,20},{20,24},{24,28},{28,32},{32,36}... | collective-permute-start | bytes 1544 | tf_op jit(solution)/shard_map/ppermute | solution.py:24
  125.8 8.5 %collective-permute-start.4 = (f32[66,1]{1,0:T(8,128)S(1)}, f32[66,1]{1,0:T(8,128)S(1)}, u32[]{:S(2)}, u32[]{:S(2)}) collective-permute-start(f32[66,1]{1,0:T(8,128)S(1)} %get-tuple-element.20), channel_id=1, source_target_pairs={{1,0},{2,1},{3,2},{5,4},{6,5},{7,6},{9,8},{10,9},{11,10},{13,12},{... | collective-permute-start | bytes 800 | tf_op jit(solution)/shard_map/ppermute | solution.py:25
  127.1 7.2 %collective-permute-start.5 = (f32[66,1]{1,0:T(8,128)S(1)}, f32[66,1]{1,0:T(8,128)S(1)}, u32[]{:S(2)}, u32[]{:S(2)}) collective-permute-start(f32[66,1]{1,0:T(8,128)S(1)} %get-tuple-element.21), channel_id=1, source_target_pairs={{0,1},{1,2},{2,3},{4,5},{5,6},{6,7},{8,9},{9,10},{10,11},{12,13},{... | collective-permute-start | bytes 800 | tf_op jit(solution)/shard_map/ppermute | solution.py:24
  134.2 95.6 %copy-start.1 = (f32[4,64,128]{2,1,0:T(8,128)}, f32[4,64,128]{2,1,0:T(8,128)S(1)}, u32[]{:S(2)}) copy-start(f32[4,64,128]{2,1,0:T(8,128)S(1)} %fusion.3) | copy-start | bytes 393220
  134.4 4.3 %collective-permute-start.6 = (f32[1,128]{1,0:T(1,128)S(1)}, f32[1,128]{1,0:T(1,128)S(1)}, u32[]{:S(2)}, u32[]{:S(2)}) collective-permute-start(f32[1,128]{1,0:T(1,128)S(1)} %get-tuple-element.35), channel_id=1, source_target_pairs={{4,0},{8,4},{12,8},{16,12},{20,16},{24,20},{28,24},{32,28},{36,32}... | collective-permute-start | bytes 1544 | tf_op jit(solution)/shard_map/ppermute | solution.py:25
  136.3 7.0 %collective-permute-start.7 = (f32[1,128]{1,0:T(1,128)S(1)}, f32[1,128]{1,0:T(1,128)S(1)}, u32[]{:S(2)}, u32[]{:S(2)}) collective-permute-start(f32[1,128]{1,0:T(1,128)S(1)} %get-tuple-element.34), channel_id=1, source_target_pairs={{0,4},{4,8},{8,12},{12,16},{16,20},{20,24},{24,28},{28,32},{32,36}... | collective-permute-start | bytes 1544 | tf_op jit(solution)/shard_map/ppermute | solution.py:24
  143.4 5.9 %collective-permute-start.10 = (f32[66,1]{1,0:T(8,128)S(1)}, f32[66,1]{1,0:T(8,128)S(1)}, u32[]{:S(2)}, u32[]{:S(2)}) collective-permute-start(f32[66,1]{1,0:T(8,128)S(1)} %get-tuple-element.18), channel_id=1, source_target_pairs={{1,0},{2,1},{3,2},{5,4},{6,5},{7,6},{9,8},{10,9},{11,10},{13,12},{... | collective-permute-start | bytes 800 | tf_op jit(solution)/shard_map/ppermute | solution.py:25
  144.7 6.2 %collective-permute-start.11 = (f32[66,1]{1,0:T(8,128)S(1)}, f32[66,1]{1,0:T(8,128)S(1)}, u32[]{:S(2)}, u32[]{:S(2)}) collective-permute-start(f32[66,1]{1,0:T(8,128)S(1)} %get-tuple-element.19), channel_id=1, source_target_pairs={{0,1},{1,2},{2,3},{4,5},{5,6},{6,7},{8,9},{9,10},{10,11},{12,13},{... | collective-permute-start | bytes 800 | tf_op jit(solution)/shard_map/ppermute | solution.py:24
  151.0 12.0 %collective-permute-start.12 = (f32[1,128]{1,0:T(1,128)S(1)}, f32[1,128]{1,0:T(1,128)S(1)}, u32[]{:S(2)}, u32[]{:S(2)}) collective-permute-start(f32[1,128]{1,0:T(1,128)S(1)} %get-tuple-element.32), channel_id=1, source_target_pairs={{0,4},{4,8},{8,12},{12,16},{16,20},{20,24},{24,28},{28,32},{32,36}... | collective-permute-start | bytes 1544 | tf_op jit(solution)/shard_map/ppermute | solution.py:24
  152.9 10.1 %collective-permute-start.13 = (f32[1,128]{1,0:T(1,128)S(1)}, f32[1,128]{1,0:T(1,128)S(1)}, u32[]{:S(2)}, u32[]{:S(2)}) collective-permute-start(f32[1,128]{1,0:T(1,128)S(1)} %get-tuple-element.33), channel_id=1, source_target_pairs={{4,0},{8,4},{12,8},{16,12},{20,16},{24,20},{28,24},{32,28},{36,32}... | collective-permute-start | bytes 1544 | tf_op jit(solution)/shard_map/ppermute | solution.py:25
  158.7 10.6 %collective-permute-start.8 = (f32[1,128]{1,0:T(1,128)S(1)}, f32[1,128]{1,0:T(1,128)S(1)}, u32[]{:S(2)}, u32[]{:S(2)}) collective-permute-start(f32[1,128]{1,0:T(1,128)S(1)} %get-tuple-element.30), channel_id=1, source_target_pairs={{4,0},{8,4},{12,8},{16,12},{20,16},{24,20},{28,24},{32,28},{36,32}... | collective-permute-start | bytes 1544 | tf_op jit(solution)/shard_map/ppermute | solution.py:25
  160.6 8.7 %collective-permute-start.9 = (f32[1,128]{1,0:T(1,128)S(1)}, f32[1,128]{1,0:T(1,128)S(1)}, u32[]{:S(2)}, u32[]{:S(2)}) collective-permute-start(f32[1,128]{1,0:T(1,128)S(1)} %get-tuple-element.31), channel_id=1, source_target_pairs={{0,4},{4,8},{8,12},{12,16},{16,20},{20,24},{24,28},{28,32},{32,36}... | collective-permute-start | bytes 1544 | tf_op jit(solution)/shard_map/ppermute | solution.py:24
  163.1 6.2 %collective-permute-start.14 = (f32[66,1]{1,0:T(8,128)S(1)}, f32[66,1]{1,0:T(8,128)S(1)}, u32[]{:S(2)}, u32[]{:S(2)}) collective-permute-start(f32[66,1]{1,0:T(8,128)S(1)} %get-tuple-element.16), channel_id=1, source_target_pairs={{1,0},{2,1},{3,2},{5,4},{6,5},{7,6},{9,8},{10,9},{11,10},{13,12},{... | collective-permute-start | bytes 800 | tf_op jit(solution)/shard_map/ppermute | solution.py:25
  164.4 6.5 %collective-permute-start.15 = (f32[66,1]{1,0:T(8,128)S(1)}, f32[66,1]{1,0:T(8,128)S(1)}, u32[]{:S(2)}, u32[]{:S(2)}) collective-permute-start(f32[66,1]{1,0:T(8,128)S(1)} %get-tuple-element.17), channel_id=1, source_target_pairs={{0,1},{1,2},{2,3},{4,5},{5,6},{6,7},{8,9},{9,10},{10,11},{12,13},{... | collective-permute-start | bytes 800 | tf_op jit(solution)/shard_map/ppermute | solution.py:24
  171.0 6.4 %collective-permute-start.16 = (f32[1,128]{1,0:T(1,128)S(1)}, f32[1,128]{1,0:T(1,128)S(1)}, u32[]{:S(2)}, u32[]{:S(2)}) collective-permute-start(f32[1,128]{1,0:T(1,128)S(1)} %get-tuple-element.29), channel_id=1, source_target_pairs={{4,0},{8,4},{12,8},{16,12},{20,16},{24,20},{28,24},{32,28},{36,32}... | collective-permute-start | bytes 1544 | tf_op jit(solution)/shard_map/ppermute | solution.py:25
  175.4 7.0 %collective-permute-start.17 = (f32[1,128]{1,0:T(1,128)S(1)}, f32[1,128]{1,0:T(1,128)S(1)}, u32[]{:S(2)}, u32[]{:S(2)}) collective-permute-start(f32[1,128]{1,0:T(1,128)S(1)} %get-tuple-element.28), channel_id=1, source_target_pairs={{0,4},{4,8},{8,12},{12,16},{16,20},{20,24},{24,28},{28,32},{32,36}... | collective-permute-start | bytes 1544 | tf_op jit(solution)/shard_map/ppermute | solution.py:24
  182.5 5.9 %collective-permute-start.20 = (f32[66,1]{1,0:T(8,128)S(1)}, f32[66,1]{1,0:T(8,128)S(1)}, u32[]{:S(2)}, u32[]{:S(2)}) collective-permute-start(f32[66,1]{1,0:T(8,128)S(1)} %get-tuple-element.14), channel_id=1, source_target_pairs={{1,0},{2,1},{3,2},{5,4},{6,5},{7,6},{9,8},{10,9},{11,10},{13,12},{... | collective-permute-start | bytes 800 | tf_op jit(solution)/shard_map/ppermute | solution.py:25
  183.8 6.2 %collective-permute-start.21 = (f32[66,1]{1,0:T(8,128)S(1)}, f32[66,1]{1,0:T(8,128)S(1)}, u32[]{:S(2)}, u32[]{:S(2)}) collective-permute-start(f32[66,1]{1,0:T(8,128)S(1)} %get-tuple-element.15), channel_id=1, source_target_pairs={{0,1},{1,2},{2,3},{4,5},{5,6},{6,7},{8,9},{9,10},{10,11},{12,13},{... | collective-permute-start | bytes 800 | tf_op jit(solution)/shard_map/ppermute | solution.py:24
  190.1 12.0 %collective-permute-start.22 = (f32[1,128]{1,0:T(1,128)S(1)}, f32[1,128]{1,0:T(1,128)S(1)}, u32[]{:S(2)}, u32[]{:S(2)}) collective-permute-start(f32[1,128]{1,0:T(1,128)S(1)} %get-tuple-element.26), channel_id=1, source_target_pairs={{0,4},{4,8},{8,12},{12,16},{16,20},{20,24},{24,28},{28,32},{32,36}... | collective-permute-start | bytes 1544 | tf_op jit(solution)/shard_map/ppermute | solution.py:24
  192.0 10.1 %collective-permute-start.23 = (f32[1,128]{1,0:T(1,128)S(1)}, f32[1,128]{1,0:T(1,128)S(1)}, u32[]{:S(2)}, u32[]{:S(2)}) collective-permute-start(f32[1,128]{1,0:T(1,128)S(1)} %get-tuple-element.27), channel_id=1, source_target_pairs={{4,0},{8,4},{12,8},{16,12},{20,16},{24,20},{28,24},{32,28},{36,32}... | collective-permute-start | bytes 1544 | tf_op jit(solution)/shard_map/ppermute | solution.py:25
  197.8 10.6 %collective-permute-start.18 = (f32[1,128]{1,0:T(1,128)S(1)}, f32[1,128]{1,0:T(1,128)S(1)}, u32[]{:S(2)}, u32[]{:S(2)}) collective-permute-start(f32[1,128]{1,0:T(1,128)S(1)} %get-tuple-element.24), channel_id=1, source_target_pairs={{4,0},{8,4},{12,8},{16,12},{20,16},{24,20},{28,24},{32,28},{36,32}... | collective-permute-start | bytes 1544 | tf_op jit(solution)/shard_map/ppermute | solution.py:25
  199.7 8.7 %collective-permute-start.19 = (f32[1,128]{1,0:T(1,128)S(1)}, f32[1,128]{1,0:T(1,128)S(1)}, u32[]{:S(2)}, u32[]{:S(2)}) collective-permute-start(f32[1,128]{1,0:T(1,128)S(1)} %get-tuple-element.25), channel_id=1, source_target_pairs={{0,4},{4,8},{8,12},{12,16},{16,20},{20,24},{24,28},{28,32},{32,36}... | collective-permute-start | bytes 1544 | tf_op jit(solution)/shard_map/ppermute | solution.py:24
  202.2 6.2 %collective-permute-start.24 = (f32[66,1]{1,0:T(8,128)S(1)}, f32[66,1]{1,0:T(8,128)S(1)}, u32[]{:S(2)}, u32[]{:S(2)}) collective-permute-start(f32[66,1]{1,0:T(8,128)S(1)} %get-tuple-element.12), channel_id=1, source_target_pairs={{1,0},{2,1},{3,2},{5,4},{6,5},{7,6},{9,8},{10,9},{11,10},{13,12},{... | collective-permute-start | bytes 800 | tf_op jit(solution)/shard_map/ppermute | solution.py:25
  203.5 6.5 %collective-permute-start.25 = (f32[66,1]{1,0:T(8,128)S(1)}, f32[66,1]{1,0:T(8,128)S(1)}, u32[]{:S(2)}, u32[]{:S(2)}) collective-permute-start(f32[66,1]{1,0:T(8,128)S(1)} %get-tuple-element.13), channel_id=1, source_target_pairs={{0,1},{1,2},{2,3},{4,5},{5,6},{6,7},{8,9},{9,10},{10,11},{12,13},{... | collective-permute-start | bytes 800 | tf_op jit(solution)/shard_map/ppermute | solution.py:24
  210.1 19.7 %copy-start.3 = (f32[64,128]{1,0:T(8,128)}, f32[64,128]{1,0:T(8,128)S(1)}, u32[]{:S(2)}) copy-start(f32[64,128]{1,0:T(8,128)S(1)} %fusion.31) | copy-start | bytes 98308
  210.2 6.4 %collective-permute-start.26 = (f32[1,128]{1,0:T(1,128)S(1)}, f32[1,128]{1,0:T(1,128)S(1)}, u32[]{:S(2)}, u32[]{:S(2)}) collective-permute-start(f32[1,128]{1,0:T(1,128)S(1)} %get-tuple-element.22), channel_id=1, source_target_pairs={{4,0},{8,4},{12,8},{16,12},{20,16},{24,20},{28,24},{32,28},{36,32}... | collective-permute-start | bytes 1544 | tf_op jit(solution)/shard_map/ppermute | solution.py:25
  214.6 7.0 %collective-permute-start.27 = (f32[1,128]{1,0:T(1,128)S(1)}, f32[1,128]{1,0:T(1,128)S(1)}, u32[]{:S(2)}, u32[]{:S(2)}) collective-permute-start(f32[1,128]{1,0:T(1,128)S(1)} %get-tuple-element.23), channel_id=1, source_target_pairs={{0,4},{4,8},{8,12},{12,16},{16,20},{20,24},{24,28},{28,32},{32,36}... | collective-permute-start | bytes 1544 | tf_op jit(solution)/shard_map/ppermute | solution.py:24
  221.6 5.9 %collective-permute-start.28 = (f32[66,1]{1,0:T(8,128)S(1)}, f32[66,1]{1,0:T(8,128)S(1)}, u32[]{:S(2)}, u32[]{:S(2)}) collective-permute-start(f32[66,1]{1,0:T(8,128)S(1)} %get-tuple-element.10), channel_id=1, source_target_pairs={{1,0},{2,1},{3,2},{5,4},{6,5},{7,6},{9,8},{10,9},{11,10},{13,12},{... | collective-permute-start | bytes 800 | tf_op jit(solution)/shard_map/ppermute | solution.py:25
  222.9 6.2 %collective-permute-start.29 = (f32[66,1]{1,0:T(8,128)S(1)}, f32[66,1]{1,0:T(8,128)S(1)}, u32[]{:S(2)}, u32[]{:S(2)}) collective-permute-start(f32[66,1]{1,0:T(8,128)S(1)} %get-tuple-element.11), channel_id=1, source_target_pairs={{0,1},{1,2},{2,3},{4,5},{5,6},{6,7},{8,9},{9,10},{10,11},{12,13},{... | collective-permute-start | bytes 800 | tf_op jit(solution)/shard_map/ppermute | solution.py:24
where the time goes:
time: 234 us; the launch traced here: 230 us
  starting transfers between devices  109 us (47%)
  local copies, waits for them, and re-layouts  65.3 us (28%)
  waiting for transfers between devices  38.5 us (16%)
  matrix products  10 us (4%)
  other arithmetic  5.86 us (3%)
    scatter x1, local copies, waits for them, and re-layouts, on_device(): jnp.zeros((devices * capacity, fields, block_width), jnp.float32)  54.7 us
    ppermute x15, starting transfers between devices, padded_2(): before = lax.ppermute(last, axis, up)  47.3 us
    ppermute x15, starting transfers between devices, padded_2(): after = lax.ppermute(initial, axis, down)  41.3 us
    ppermute x15, waiting for transfers between devices, padded_2(): before = lax.ppermute(last, axis, up)  38.5 us
    all_to_all x1, starting transfers between devices, on_device(): lax.all_to_all(labels, ('atm', 'ocn'), split_axis=0, concat_axis=0, tiled...  10.5 us
    all_to_all x1, starting transfers between devices, on_device(): lax.all_to_all(buffer, ('atm', 'ocn'), split_axis=0, concat_axis=0, tiled...  9.76 us
    dot_general x1, matrix products, on_device(): jnp.einsum('fwb,wbc->wfc', picked, remap_weights, preferred_element_type=...  8.97 us
  transfers between devices with their start and end apart: 32, of which 9 were waited for; matrix products, arithmetic and copies ran while one was open for 31% of the time, Pallas kernels for 0%

commit v1 on v0

v1 whole, which is shorter than its diff:
```python
import functools

import jax
import jax.numpy as jnp
from jax import lax
from jax.experimental import pallas as pl
from jax.experimental.pallas import tpu as pltpu
from jax.sharding import PartitionSpec as P

CX = 64
STEPS = 3
F = 4
B = 128
CAP = 9
ROWS = 40
LABEL_ROW = 39
EDGE = 5
REACH = 6
CHUNKS = 16

courant = 0.5
forcing = 0.3
coriolis = 0.2
damping = 0.05
steric = 0.5

AXES = ("atm", "ocn")


def pack_kernel(
    owner_h,
    target_h,
    block_h,
    src_h,
    weights_h,
    out,
    weights,
    lhs,
    labels,
    src,
    owner,
    target,
    block,
    count,
    sems,
    small_sems,
    *,
    devices,
    ocn,
):
    total = weights.shape[0]
    per = total // CHUNKS
    smalls = [
        pltpu.make_async_copy(a, b, small_sems.at[i])
        for i, (a, b) in enumerate(
            ((src_h, src), (owner_h, owner), (target_h, target), (block_h, block))
        )
    ]
    for copy in smalls:
        copy.start()
    copies = [
        pltpu.make_async_copy(
            weights_h.at[pl.ds(c * per, per)], weights.at[pl.ds(c * per, per)], sems.at[c]
        )
        for c in range(CHUNKS)
    ]
    for copy in copies:
        copy.start()
    out[...] = jnp.zeros(out.shape, jnp.float32)
    labels[...] = jnp.full(labels.shape, -1.0, jnp.float32)

    def clear(i, carry):
        count[i] = 0
        return carry

    lax.fori_loop(0, devices, clear, 0, unroll=8)
    smalls[0].wait()
    zero = jnp.zeros((F, B), jnp.float32)
    for b in range(src.shape[1] // B):
        value = src[:, b * B : (b + 1) * B].astype(jnp.float32)
        for j in range(4):
            parts = [zero] * 4
            parts[j] = value
            lhs[j, b] = jnp.concatenate(parts, 0).astype(jnp.bfloat16)
    for copy in smalls[1:]:
        copy.wait()
    lane = lax.broadcasted_iota(jnp.int32, (1, B), 1)
    for c in range(CHUNKS):
        copies[c].wait()
        for w in range(c * per, (c + 1) * per, 4):
            left = jnp.concatenate([lhs[j, block[w + j]] for j in range(4)], axis=1)
            right = weights[w : w + 4].reshape(4 * B, B)
            rows = jnp.dot(left, right, preferred_element_type=jnp.float32)
            for j in range(4):
                o = owner[w + j]
                k = count[o]
                count[o] = k + 1
                out[pl.ds(o * ROWS + k * F, F), :] = rows[F * j : F * (j + 1)]
                labels[pl.ds(o, 1), :] = jnp.where(
                    lane == k, target[w + j].astype(jnp.float32), labels[pl.ds(o, 1), :]
                )

    lane = lax.broadcasted_iota(jnp.int32, (devices, B), 1)
    edge = [jnp.zeros((devices, B), jnp.float32) for _ in range(4)]
    for k in range(CAP):
        late = k >= 6
        for f in range(F):
            at = (k - 6 if late else k) * F * EDGE + f * EDGE
            here = (lane >= at) & (lane < at + EDGE)
            column = out[pl.ds(k * F + f, devices, stride=ROWS), :]
            last = pltpu.roll(column, (at - (B - EDGE)) % B, 1)
            first = pltpu.roll(column, at, 1) if at else column
            edge[2 * late] = jnp.where(here, last, edge[2 * late])
            edge[2 * late + 1] = jnp.where(here, first, edge[2 * late + 1])
    last, first, last_late, first_late = edge
    out[pl.ds(36, devices, stride=ROWS), :] = pltpu.roll(last, 1, 0)
    late = jnp.where(
        lane < 64,
        pltpu.roll(last_late, 1, 0),
        pltpu.roll(pltpu.roll(first_late, devices - 1, 0), 64, 1),
    )
    out[pl.ds(37, devices, stride=ROWS), :] = late
    out[pl.ds(38, devices, stride=ROWS), :] = pltpu.roll(first, devices - 1, 0)
    place = lax.broadcasted_iota(jnp.int32, (devices, B), 0) % ocn
    own = labels[...]
    before = jnp.where(place > 0, pltpu.roll(pltpu.roll(own, 1, 0), 16, 1), -1.0)
    after = jnp.where(place < ocn - 1, pltpu.roll(pltpu.roll(own, devices - 1, 0), 32, 1), -1.0)
    out[pl.ds(LABEL_ROW, devices, stride=ROWS), :] = jnp.where(
        lane < 16, own, jnp.where(lane < 32, before, jnp.where(lane < 48, after, -1.0))
    )


def pack(owner, target, block, src, weights, devices, ocn):
    total = weights.shape[0]
    here = pl.BlockSpec(memory_space=pltpu.HBM)
    return pl.pallas_call(
        functools.partial(pack_kernel, devices=devices, ocn=ocn),
        out_shape=jax.ShapeDtypeStruct((devices * ROWS, B), jnp.float32),
        in_specs=[here] * 5,
        out_specs=pl.BlockSpec(memory_space=pltpu.VMEM),
        scratch_shapes=[
            pltpu.VMEM(weights.shape, jnp.bfloat16),
            pltpu.VMEM((4, src.shape[1] // B, 4 * F, B), jnp.bfloat16),
            pltpu.VMEM((devices, B), jnp.float32),
            pltpu.VMEM(src.shape, jnp.bfloat16),
            pltpu.SMEM((total,), jnp.int32),
            pltpu.SMEM((total,), jnp.int32),
            pltpu.SMEM((total,), jnp.int32),
            pltpu.SMEM((devices,), jnp.int32),
            pltpu.SemaphoreType.DMA((CHUNKS,)),
            pltpu.SemaphoreType.DMA((4,)),
        ],
        compiler_params=pltpu.CompilerParams(vmem_limit_bytes=48 << 20),
        cost_estimate=pl.CostEstimate(
            flops=2 * F * weights.size, bytes_accessed=2 * weights.size, transcendentals=0
        ),
        name="remap_pack",
    )(owner, target, block, src, weights)


def doubled(value):
    high = value.astype(jnp.bfloat16)
    low = (value - high.astype(jnp.float32)).astype(jnp.bfloat16)
    return jnp.concatenate([high, low], axis=0)


def sum_kernel(arrived, flux, wide, first_rows, last_rows, *, devices):
    names = arrived[pl.ds(LABEL_ROW, devices, stride=ROWS), :].T
    row = lax.broadcasted_iota(jnp.int32, (CX, devices), 0).astype(jnp.float32)

    def pick(lane):
        hot = (row == names[lane : lane + 1, :]).astype(jnp.bfloat16)
        return jnp.concatenate([hot, hot], axis=1)

    total = jnp.zeros((CX, F * B), jnp.float32)
    for k in range(CAP):
        rows = jnp.concatenate(
            [
                doubled(arrived[pl.ds(k * F + f, devices, stride=ROWS), :])
                for f in range(F)
            ],
            axis=1,
        )
        total = total + jnp.dot(pick(k), rows, preferred_element_type=jnp.float32)

    def edges(at, picks):
        rows = doubled(arrived[pl.ds(at, devices, stride=ROWS), :])
        return jnp.dot(jnp.concatenate(picks, 0), rows, preferred_element_type=jnp.float32)

    before = edges(36, [pick(16 + k) for k in range(6)])
    late = edges(37, [pick(16 + k) for k in range(6, 9)] + [pick(32 + k) for k in range(6, 9)])
    after = edges(38, [pick(32 + k) for k in range(6)])

    def shifted(value, k, by):
        return pltpu.roll(value[k * CX : (k + 1) * CX], by % B, 1)

    last = before[:CX]
    first = after[:CX]
    for k in range(1, 6):
        last = last + shifted(before, k, -20 * k)
        first = first + shifted(after, k, -20 * k)
    for k in range(3):
        last = last + shifted(late, k, -20 * k)
        first = first + shifted(late, 3 + k, -64 - 20 * k)
    lane = lax.broadcasted_iota(jnp.int32, (CX, B), 1)
    sides = []
    for f in range(F):
        low = pltpu.roll(last, (B - EDGE - EDGE * f) % B, 1)
        high = pltpu.roll(first, (B - EDGE * f) % B, 1) if f else first
        sides.append(jnp.where(lane >= B - EDGE, low, jnp.where(lane < EDGE, high, 0.0)))
    own = [total[:, f * B : (f + 1) * B] for f in range(F)]
    for f in range(F):
        flux[f] = own[f]
    fields = [
        jnp.concatenate([own[0], sides[0]], axis=1),
        jnp.concatenate([own[1], sides[1]], axis=1),
        jnp.concatenate(
            [
                forcing * (own[2] + steric * own[3]),
                forcing * (sides[2] + steric * sides[3]),
            ],
            axis=1,
        ),
    ]
    for i, field in enumerate(fields):
        wide[i] = field
        first_rows[i] = field[:8]
        last_rows[i] = field[CX - 8 :]


def sum_rows(arrived, devices):
    inside = pl.BlockSpec(memory_space=pltpu.VMEM)
    return pl.pallas_call(
        functools.partial(sum_kernel, devices=devices),
        out_shape=(
            jax.ShapeDtypeStruct((F, CX, B), jnp.float32),
            jax.ShapeDtypeStruct((3, CX, 2 * B), jnp.float32),
            jax.ShapeDtypeStruct((3, 8, 2 * B), jnp.float32),
            jax.ShapeDtypeStruct((3, 8, 2 * B), jnp.float32),
        ),
        in_specs=[inside],
        out_specs=(inside,) * 4,
        compiler_params=pltpu.CompilerParams(vmem_limit_bytes=32 << 20),
        name="sum_rows",
    )(arrived)


def step_kernel(state, wide, above, below, height_out, zonal_out, merid_out):
    rows = CX + 16

    def field(i):
        return jnp.concatenate([above[i], wide[i], below[i]], axis=0)

    zonal_flux, merid_flux, source = field(0), field(1), field(2)
    height, zonal, merid, depth = state[0], state[1], state[2], state[3]
    inside = depth > 0.0

    def grad_x(a):
        return 0.5 * (pltpu.roll(a, rows - 1, 0) - pltpu.roll(a, 1, 0))

    def grad_y(a):
        return 0.5 * (pltpu.roll(a, 2 * B - 1, 1) - pltpu.roll(a, 1, 1))

    for _ in range(STEPS):
        height = height - courant * depth * (grad_x(zonal) + grad_y(merid)) + source
        new_zonal = (
            zonal
            - courant * grad_x(height)
            + coriolis * merid
            + forcing * zonal_flux
            - damping * zonal
        )
        new_merid = (
            merid
            - courant * grad_y(height)
            - coriolis * zonal
            + forcing * merid_flux
            - damping * merid
        )
        zonal = jnp.where(inside, new_zonal, 0.0)
        merid = jnp.where(inside, new_merid, 0.0)
    height_out[...] = height[8 : 8 + CX, :B]
    zonal_out[...] = zonal[8 : 8 + CX, :B]
    merid_out[...] = merid[8 : 8 + CX, :B]


def substeps(state, wide, above, below):
    inside = pl.BlockSpec(memory_space=pltpu.VMEM)
    shape = jax.ShapeDtypeStruct((CX, B), jnp.float32)
    return pl.pallas_call(
        step_kernel,
        out_shape=(shape,) * 3,
        in_specs=[inside] * 4,
        out_specs=(inside,) * 3,
        compiler_params=pltpu.CompilerParams(vmem_limit_bytes=32 << 20),
        name="substeps",
    )(state, wide, above, below)


def from_before(x, axis):
    n = lax.axis_size(axis)
    return lax.ppermute(x, axis, [(i, i + 1) for i in range(n - 1)])


def from_after(x, axis):
    n = lax.axis_size(axis)
    return lax.ppermute(x, axis, [(i + 1, i) for i in range(n - 1)])


def on_device(
    source_flux,
    remap_weights,
    source_block,
    owner_device,
    target_row,
    sea_height,
    u_velocity,
    v_velocity,
    ocean_depth,
):
    ocn = lax.axis_size("ocn")
    devices = lax.axis_size("atm") * ocn
    messages = pack(
        owner_device[:, 0], target_row, source_block, source_flux, remap_weights, devices, ocn
    )
    arrived = lax.all_to_all(messages, AXES, split_axis=0, concat_axis=0, tiled=True)

    state = jnp.stack([sea_height, u_velocity, v_velocity, ocean_depth])
    state, messages = lax.optimization_barrier((state, messages))
    before = from_before(state[:, :, B - REACH :], "ocn")
    after = from_after(state[:, :, :REACH], "ocn")
    gap = jnp.zeros((4, CX, B - 2 * REACH), jnp.float32)
    state = jnp.concatenate([state, after, gap, before], axis=2)
    above = from_before(state[:, CX - 8 :], "atm")
    below = from_after(state[:, :8], "atm")
    state = jnp.concatenate([above, state, below], axis=1)

    flux, wide, first_rows, last_rows = sum_rows(arrived, devices)
    above = from_before(last_rows, "atm")
    below = from_after(first_rows, "atm")
    height, zonal, merid = substeps(state, wide, above, below)
    return flux, height, zonal, merid


def solution(mesh):
    placed = (
        P(None, AXES),
        P(AXES, None, None),
        P(AXES),
        P(AXES, None),
        P(AXES),
        P("atm", "ocn"),
        P("atm", "ocn"),
        P("atm", "ocn"),
        P("atm", "ocn"),
    )
    return jax.shard_map(
        on_device,
        mesh=mesh,
        in_specs=placed,
        out_specs=(P(None, "atm", "ocn"), P("atm", "ocn"), P("atm", "ocn"), P("atm", "ocn")),
        check_vma=False,
    )
```

time: 234 us -> 78.6 us (0.34)
  the two profiles are of different devices: /device:TPU:4 before, /device:TPU:59 now
where the time goes in v1:
time: 78.6 us; the launch traced here: 78.1 us
  waiting for transfers between devices  32.2 us (41%)
  starting transfers between devices  29.4 us (37%)
  Pallas kernels  12.5 us (16%)
  local copies, waits for them, and re-layouts  2.21 us (3%)
  other arithmetic  0.93 us (1%)
  between operations  0.83 us (1%)
    ppermute x3, waiting for transfers between devices, from_after(): return lax.ppermute(x, axis, [(i + 1, i) for i in range(n - 1)])  32.2 us
    ppermute x3, starting transfers between devices, from_before(): return lax.ppermute(x, axis, [(i, i + 1) for i in range(n - 1)])  13.2 us
    all_to_all x1, starting transfers between devices, on_device(): lax.all_to_all(messages, AXES, split_axis=0, concat_axis=0, tiled=True)  10.4 us
    pallas_call x1, Pallas kernels, pack(): pl.pallas_call(functools.partial(pack_kernel, devices=devices, ocn=ocn),...  9.82 us
    ppermute x3, starting transfers between devices, from_after(): return lax.ppermute(x, axis, [(i + 1, i) for i in range(n - 1)])  5.76 us
    unnamed x14, local copies, waits for them, and re-layouts  2.11 us
  transfers between devices with their start and end apart: 7, of which 2 were waited for; matrix products, arithmetic and copies ran while one was open for 0% of the time, Pallas kernels for 2%

profile of v1, /device:TPU:59, one launch (start us, length us, event | category | flops | bytes accessed | tf_op | source)
XLA Modules:
  0.0 78.1 jit_solution(11792287169262167646)
XLA Ops:
  0.6 0.7 reduce.owner_h
  1.3 0.0 copy-start
  1.3 0.7 copy-done
  2.1 0.0 copy-start.1
  2.1 0.7 copy-done.1
  2.7 0.0 copy-start.2
  2.7 0.7 copy-done.2
  3.4 9.8 %remap_pack.1 = f32[5120,128]{1,0:T(8,128)} custom-call(s32[576]{0:T(1024)S(1)} %reduce.owner_h, s32[576]{0:T(1024)S(1)} %copy-done.1, s32[576]{0:T(1024)S(1)} %copy-done.2, bf16[4,2048]{1,0:T(4,128)(2,1)S(1)} %copy-done, bf16[576,128,128]{2,1,0:T(8,128)(2,1)} %weights_h.1), custom_call_target="tpu_custom_call" | custom-call | flops 75497472 | bytes 18874368 | tf_op jit(solution)/shard_map/remap_pack/pallas_call | solution.py:136
  13.3 0.0 copy-start.3
  13.3 0.0 copy-start.4
  13.3 0.0 copy-start.5
  13.3 0.0 copy-start.6
  13.3 10.4 %all-to-all-start = ((f32[128,40,128]{2,1,0:T(8,128)}), f32[128,40,128]{2,1,0:T(8,128)S(1)}, u32[]{:S(2)}, u32[]{:S(2)}) async-start(f32[128,40,128]{2,1,0:T(8,128)} %bitcast), calls=%async_computation | async-start | bytes 5242880 | tf_op jit(solution)/shard_map/all_to_all | solution.py:326
  23.7 0.0 copy-done.3
  23.7 0.0 copy-done.4
  23.7 0.0 copy-done.5
  23.7 0.0 copy-done.6
  23.8 0.1 fusion
  23.9 1.9 %collective-permute-start = (f32[4,64,6]{2,1,0:T(8,128)S(1)}, f32[4,64,6]{2,1,0:T(8,128)S(1)}, u32[]{:S(2)}, u32[]{:S(2)}) collective-permute-start(f32[4,64,6]{2,1,0:T(8,128)S(1)} %get-tuple-element.22), channel_id=1, source_target_pairs={{1,0},{2,1},{3,2},{5,4},{6,5},{7,6},{9,8},{10,9},{11,10},{13,12},{... | collective-permute-start | bytes 18440 | tf_op jit(solution)/shard_map/ppermute | solution.py:307
  25.8 3.4 %collective-permute-start.1 = (f32[4,64,6]{2,1,0:T(8,128)S(1)}, f32[4,64,6]{2,1,0:T(8,128)S(1)}, u32[]{:S(2)}, u32[]{:S(2)}) collective-permute-start(f32[4,64,6]{2,1,0:T(8,128)S(1)} %get-tuple-element.23), channel_id=1, source_target_pairs={{0,1},{1,2},{2,3},{4,5},{5,6},{6,7},{8,9},{9,10},{10,11},{12,13},{... | collective-permute-start | bytes 18440 | tf_op jit(solution)/shard_map/ppermute | solution.py:302
  29.2 27.1 %collective-permute-done = f32[4,64,6]{2,1,0:T(8,128)S(1)} collective-permute-done((f32[4,64,6]{2,1,0:T(8,128)S(1)}, f32[4,64,6]{2,1,0:T(8,128)S(1)}, u32[]{:S(2)}, u32[]{:S(2)}) %collective-permute-start) | collective-permute-done | bytes 6176 | tf_op jit(solution)/shard_map/ppermute | solution.py:307
  56.2 0.0 collective-permute-done.1
  56.2 0.1 pad_maximum_fusion.5
  56.3 4.1 %collective-permute-start.2 = (f32[4,8,256]{2,1,0:T(8,128)S(1)}, f32[4,8,256]{2,1,0:T(8,128)S(1)}, u32[]{:S(2)}, u32[]{:S(2)}) collective-permute-start(f32[4,8,256]{2,1,0:T(8,128)S(1)} %get-tuple-element.20), channel_id=1, source_target_pairs={{0,4},{4,8},{8,12},{12,16},{16,20},{20,24},{24,28},{28,32},{32,36}... | collective-permute-start | bytes 98312 | tf_op jit(solution)/shard_map/ppermute | solution.py:302
  60.4 1.9 %collective-permute-start.3 = (f32[4,8,256]{2,1,0:T(8,128)S(1)}, f32[4,8,256]{2,1,0:T(8,128)S(1)}, u32[]{:S(2)}, u32[]{:S(2)}) collective-permute-start(f32[4,8,256]{2,1,0:T(8,128)S(1)} %get-tuple-element.21), channel_id=1, source_target_pairs={{4,0},{8,4},{12,8},{16,12},{20,16},{24,20},{28,24},{32,28},{36,32}... | collective-permute-start | bytes 98312 | tf_op jit(solution)/shard_map/ppermute | solution.py:307
  62.4 0.0 all-to-all-done
  62.4 1.4 %sum_rows.1 = (f32[4,64,128]{2,1,0:T(8,128)}, f32[3,64,256]{2,1,0:T(8,128)S(1)}, f32[3,8,256]{2,1,0:T(8,128)S(1)}, f32[3,8,256]{2,1,0:T(8,128)S(1)}) custom-call(f32[5120,128]{1,0:T(8,128)S(1)} %bitcast.6), custom_call_target="tpu_custom_call" | custom-call | tf_op jit(solution)/shard_map/sum_rows/pallas_call | solution.py:233
  63.8 5.7 %collective-permute-start.4 = (f32[3,8,256]{2,1,0:T(8,128)S(1)}, f32[3,8,256]{2,1,0:T(8,128)S(1)}, u32[]{:S(2)}, u32[]{:S(2)}) collective-permute-start(f32[3,8,256]{2,1,0:T(8,128)S(1)} %get-tuple-element.15), channel_id=1, source_target_pairs={{0,4},{4,8},{8,12},{12,16},{16,20},{20,24},{24,28},{28,32},{32,36}... | collective-permute-start | bytes 73736 | tf_op jit(solution)/shard_map/ppermute | solution.py:302
  69.5 1.9 %collective-permute-start.5 = (f32[3,8,256]{2,1,0:T(8,128)S(1)}, f32[3,8,256]{2,1,0:T(8,128)S(1)}, u32[]{:S(2)}, u32[]{:S(2)}) collective-permute-start(f32[3,8,256]{2,1,0:T(8,128)S(1)} %get-tuple-element.16), channel_id=1, source_target_pairs={{4,0},{8,4},{12,8},{16,12},{20,16},{24,20},{28,24},{32,28},{36,32}... | collective-permute-start | bytes 73736 | tf_op jit(solution)/shard_map/ppermute | solution.py:307
  71.5 0.0 collective-permute-done.2
  71.5 0.0 collective-permute-done.3
  71.5 0.1 pad_maximum_fusion.state
  71.6 0.0 collective-permute-done.4.above
  71.6 5.2 %collective-permute-done.5.below = f32[3,8,256]{2,1,0:T(8,128)S(1)} collective-permute-done((f32[3,8,256]{2,1,0:T(8,128)S(1)}, f32[3,8,256]{2,1,0:T(8,128)S(1)}, u32[]{:S(2)}, u32[]{:S(2)}) %collective-permute-start.5) | collective-permute-done | bytes 24608 | tf_op jit(solution)/shard_map/ppermute | solution.py:307
  76.8 1.3 %substeps.1 = (f32[64,128]{1,0:T(8,128)}, f32[64,128]{1,0:T(8,128)}, f32[64,128]{1,0:T(8,128)}) custom-call(f32[4,80,256]{2,1,0:T(8,128)S(1)} %pad_maximum_fusion.state, f32[3,64,256]{2,1,0:T(8,128)S(1)} %get-tuple-element.14.wide, f32[3,8,256]{2,1,0:T(8,128)S(1)} %collective-permute-done.4.above, f32[3,8,256]{2,1,0:T(8,128)S(1)} %collective-permute-done.5.below), custom_call_target="tpu_custom_call" | custom-call | tf_op jit(solution)/shard_map/substeps/pallas_call | solution.py:290
  (2 shorter events, 0.0 us)
Async XLA Ops:
  1.3 0.7 copy-start
  2.1 0.7 copy-start.1
  2.7 0.7 copy-start.2
  13.3 10.5 %copy-start.3 = (f32[64,128]{1,0:T(8,128)S(1)}, f32[64,128]{1,0:T(8,128)}, u32[]{:S(2)}) copy-start(f32[64,128]{1,0:T(8,128)} %param.17) | copy-start | bytes 98308
  13.3 10.4 %copy-start.4 = (f32[64,128]{1,0:T(8,128)S(1)}, f32[64,128]{1,0:T(8,128)}, u32[]{:S(2)}) copy-start(f32[64,128]{1,0:T(8,128)} %param.16) | copy-start | bytes 98308
  13.3 10.4 %copy-start.5 = (f32[64,128]{1,0:T(8,128)S(1)}, f32[64,128]{1,0:T(8,128)}, u32[]{:S(2)}) copy-start(f32[64,128]{1,0:T(8,128)} %param.15) | copy-start | bytes 98308
  13.3 10.4 %copy-start.6 = (f32[64,128]{1,0:T(8,128)S(1)}, f32[64,128]{1,0:T(8,128)}, u32[]{:S(2)}) copy-start(f32[64,128]{1,0:T(8,128)} %param.14) | copy-start | bytes 98308
  13.3 49.1 %all-to-all-start = ((f32[128,40,128]{2,1,0:T(8,128)}), f32[128,40,128]{2,1,0:T(8,128)S(1)}, u32[]{:S(2)}, u32[]{:S(2)}) async-start(f32[128,40,128]{2,1,0:T(8,128)} %bitcast), calls=%async_computation | async-start | bytes 5242880 | tf_op jit(solution)/shard_map/all_to_all | solution.py:326
  23.9 32.4 %collective-permute-start = (f32[4,64,6]{2,1,0:T(8,128)S(1)}, f32[4,64,6]{2,1,0:T(8,128)S(1)}, u32[]{:S(2)}, u32[]{:S(2)}) collective-permute-start(f32[4,64,6]{2,1,0:T(8,128)S(1)} %get-tuple-element.22), channel_id=1, source_target_pairs={{1,0},{2,1},{3,2},{5,4},{6,5},{7,6},{9,8},{10,9},{11,10},{13,12},{... | collective-permute-start | bytes 18440 | tf_op jit(solution)/shard_map/ppermute | solution.py:307
  25.8 30.4 %collective-permute-start.1 = (f32[4,64,6]{2,1,0:T(8,128)S(1)}, f32[4,64,6]{2,1,0:T(8,128)S(1)}, u32[]{:S(2)}, u32[]{:S(2)}) collective-permute-start(f32[4,64,6]{2,1,0:T(8,128)S(1)} %get-tuple-element.23), channel_id=1, source_target_pairs={{0,1},{1,2},{2,3},{4,5},{5,6},{6,7},{8,9},{9,10},{10,11},{12,13},{... | collective-permute-start | bytes 18440 | tf_op jit(solution)/shard_map/ppermute | solution.py:302
  56.3 15.1 %collective-permute-start.2 = (f32[4,8,256]{2,1,0:T(8,128)S(1)}, f32[4,8,256]{2,1,0:T(8,128)S(1)}, u32[]{:S(2)}, u32[]{:S(2)}) collective-permute-start(f32[4,8,256]{2,1,0:T(8,128)S(1)} %get-tuple-element.20), channel_id=1, source_target_pairs={{0,4},{4,8},{8,12},{12,16},{16,20},{20,24},{24,28},{28,32},{32,36}... | collective-permute-start | bytes 98312 | tf_op jit(solution)/shard_map/ppermute | solution.py:302
  60.4 11.0 %collective-permute-start.3 = (f32[4,8,256]{2,1,0:T(8,128)S(1)}, f32[4,8,256]{2,1,0:T(8,128)S(1)}, u32[]{:S(2)}, u32[]{:S(2)}) collective-permute-start(f32[4,8,256]{2,1,0:T(8,128)S(1)} %get-tuple-element.21), channel_id=1, source_target_pairs={{4,0},{8,4},{12,8},{16,12},{20,16},{24,20},{28,24},{32,28},{36,32}... | collective-permute-start | bytes 98312 | tf_op jit(solution)/shard_map/ppermute | solution.py:307
  63.8 7.8 %collective-permute-start.4 = (f32[3,8,256]{2,1,0:T(8,128)S(1)}, f32[3,8,256]{2,1,0:T(8,128)S(1)}, u32[]{:S(2)}, u32[]{:S(2)}) collective-permute-start(f32[3,8,256]{2,1,0:T(8,128)S(1)} %get-tuple-element.15), channel_id=1, source_target_pairs={{0,4},{4,8},{8,12},{12,16},{16,20},{20,24},{24,28},{28,32},{32,36}... | collective-permute-start | bytes 73736 | tf_op jit(solution)/shard_map/ppermute | solution.py:302
  69.5 7.3 %collective-permute-start.5 = (f32[3,8,256]{2,1,0:T(8,128)S(1)}, f32[3,8,256]{2,1,0:T(8,128)S(1)}, u32[]{:S(2)}, u32[]{:S(2)}) collective-permute-start(f32[3,8,256]{2,1,0:T(8,128)S(1)} %get-tuple-element.16), channel_id=1, source_target_pairs={{4,0},{8,4},{12,8},{16,12},{20,16},{24,20},{28,24},{32,28},{36,32}... | collective-permute-start | bytes 73736 | tf_op jit(solution)/shard_map/ppermute | solution.py:307

commit v2 on v1

v2 whole, which is shorter than its diff:
```python
import functools

import jax
import jax.numpy as jnp
from jax import lax
from jax.experimental import pallas as pl
from jax.experimental.pallas import tpu as pltpu
from jax.sharding import PartitionSpec as P

CX = 64
STEPS = 3
F = 4
B = 128
CAP = 9
ROWS = 38
REACH = 6
SPANS = ((0, 3), (6, 4), (14, 5))
SPAN = 24
SPLIT = 5
LABELS = 96
CHUNKS = 16

courant = 0.5
forcing = 0.3
coriolis = 0.2
damping = 0.05
steric = 0.5

AXES = ("atm", "ocn")


def pack_kernel(
    owner_h,
    target_h,
    block_h,
    src_h,
    weights_h,
    out,
    weights,
    lhs,
    labels,
    src,
    owner,
    target,
    block,
    count,
    built,
    sems,
    small_sems,
    out_sems,
    *,
    devices,
    ocn,
):
    total = weights.shape[0]
    per = total // CHUNKS
    smalls = [
        pltpu.make_async_copy(a, b, small_sems.at[i])
        for i, (a, b) in enumerate(
            ((src_h, src), (owner_h, owner), (target_h, target), (block_h, block))
        )
    ]
    for copy in smalls:
        copy.start()
    copies = [
        pltpu.make_async_copy(
            weights_h.at[pl.ds(c * per, per)], weights.at[pl.ds(c * per, per)], sems.at[c]
        )
        for c in range(CHUNKS)
    ]
    copies[0].start()
    built[...] = jnp.zeros(built.shape, jnp.float32)
    labels[...] = jnp.full(labels.shape, -1.0, jnp.float32)

    def clear(i, carry):
        count[i] = 0
        return carry

    lax.fori_loop(0, devices, clear, 0, unroll=8)
    smalls[0].wait()
    zero = jnp.zeros((F, B), jnp.float32)
    for b in range(src.shape[1] // B):
        value = src[:, b * B : (b + 1) * B].astype(jnp.float32)
        for j in range(4):
            parts = [zero] * 4
            parts[j] = value
            lhs[j, b] = jnp.concatenate(parts, 0).astype(jnp.bfloat16)
    for copy in smalls[1:]:
        copy.wait()
    for copy in copies[1:]:
        copy.start()
    lane = lax.broadcasted_iota(jnp.int32, (1, B), 1)
    for c in range(CHUNKS):
        copies[c].wait()
        for w in range(c * per, (c + 1) * per, 4):
            left = jnp.concatenate([lhs[j, block[w + j]] for j in range(4)], axis=1)
            right = weights[w : w + 4].reshape(4 * B, B)
            rows = jnp.dot(left, right, preferred_element_type=jnp.float32)
            for j in range(4):
                o = owner[w + j]
                k = count[o]
                count[o] = k + 1
                built[pl.ds(o * ROWS + k * F, F), :] = rows[F * j : F * (j + 1)]
                labels[pl.ds(o, 1), :] = jnp.where(
                    lane == k, target[w + j].astype(jnp.float32), labels[pl.ds(o, 1), :]
                )

    group = 8 * ocn
    lane = lax.broadcasted_iota(jnp.int32, (group, B), 1)
    place = lax.broadcasted_iota(jnp.int32, (group, B), 0) % ocn
    sends = []
    for g in range(devices // group):
        base = g * group * ROWS
        edge = [jnp.zeros((group, B), jnp.float32) for _ in range(2)]
        from_before = [lane < 0, lane < 0]
        for k in range(CAP):
            part = k // SPLIT
            rows = [built[pl.ds(base + k * F + f, group, stride=ROWS), :] for f in range(F)]
            rows = [rows[0], rows[1], forcing * (rows[2] + steric * rows[3])]
            for (start, width), value in zip(SPANS, rows):
                at = (k % SPLIT) * SPAN + start
                moved = pltpu.roll(value, (at - (B - width)) % B, 1)
                edge[part] = jnp.where((lane >= at) & (lane < at + 2 * width), moved, edge[part])
                from_before[part] |= (lane >= at) & (lane < at + width)
        sides = [
            jnp.where(mask, pltpu.roll(value, 1, 0), pltpu.roll(value, group - 1, 0))
            for mask, value in zip(from_before, edge)
        ]
        own = labels[pl.ds(g * group, group), :]
        before = jnp.where(place > 0, pltpu.roll(own, 1, 0), -1.0)
        after = jnp.where(place < ocn - 1, pltpu.roll(own, group - 1, 0), -1.0)
        for i, names in enumerate((own, before, after)):
            at = LABELS + CAP * i
            sides[1] = jnp.where(
                (lane >= at) & (lane < at + CAP), pltpu.roll(names, at, 1), sides[1]
            )
        built[pl.ds(base + 36, group, stride=ROWS), :] = sides[0]
        built[pl.ds(base + 37, group, stride=ROWS), :] = sides[1]
        span = pl.ds(base, group * ROWS)
        send = pltpu.make_async_copy(built.at[span], out.at[span], out_sems.at[g])
        send.start()
        sends.append(send)
    for send in sends:
        send.wait()


def pack(owner, target, block, src, weights, devices, ocn):
    total = weights.shape[0]
    here = pl.BlockSpec(memory_space=pltpu.HBM)
    return pl.pallas_call(
        functools.partial(pack_kernel, devices=devices, ocn=ocn),
        out_shape=jax.ShapeDtypeStruct((devices * ROWS, B), jnp.float32),
        in_specs=[here] * 5,
        out_specs=here,
        scratch_shapes=[
            pltpu.VMEM(weights.shape, jnp.bfloat16),
            pltpu.VMEM((4, src.shape[1] // B, 4 * F, B), jnp.bfloat16),
            pltpu.VMEM((devices, B), jnp.float32),
            pltpu.VMEM(src.shape, jnp.bfloat16),
            pltpu.SMEM((total,), jnp.int32),
            pltpu.SMEM((total,), jnp.int32),
            pltpu.SMEM((total,), jnp.int32),
            pltpu.SMEM((devices,), jnp.int32),
            pltpu.VMEM((devices * ROWS, B), jnp.float32),
            pltpu.SemaphoreType.DMA((CHUNKS,)),
            pltpu.SemaphoreType.DMA((4,)),
            pltpu.SemaphoreType.DMA((devices // (8 * ocn),)),
        ],
        compiler_params=pltpu.CompilerParams(vmem_limit_bytes=60 << 20),
        cost_estimate=pl.CostEstimate(
            flops=2 * F * weights.size, bytes_accessed=2 * weights.size, transcendentals=0
        ),
        name="remap_pack",
    )(owner, target, block, src, weights)


def doubled(value):
    high = value.astype(jnp.bfloat16)
    low = (value - high.astype(jnp.float32)).astype(jnp.bfloat16)
    return jnp.concatenate([high, low], axis=0)


def sum_kernel(parity, arrived, state, flux, wide, to_pair, to_beside, *, devices):
    names = arrived[pl.ds(37, devices, stride=ROWS), :].T
    row = lax.broadcasted_iota(jnp.int32, (CX, devices), 0).astype(jnp.float32)

    def pick(lane):
        hot = (row == names[lane : lane + 1, :]).astype(jnp.bfloat16)
        return jnp.concatenate([hot, hot], axis=1)

    total = jnp.zeros((CX, F * B), jnp.float32)
    for k in range(CAP):
        rows = jnp.concatenate(
            [
                doubled(arrived[pl.ds(k * F + f, devices, stride=ROWS), :])
                for f in range(F)
            ],
            axis=1,
        )
        total = total + jnp.dot(pick(LABELS + k), rows, preferred_element_type=jnp.float32)

    rows = jnp.concatenate(
        [doubled(arrived[pl.ds(at, devices, stride=ROWS), :]) for at in (36, 37)], axis=0
    )
    none = jnp.zeros((CX, 2 * devices), jnp.bfloat16)
    sums = []
    for side in (LABELS + CAP, LABELS + 2 * CAP):
        hot = jnp.concatenate(
            [
                jnp.concatenate(
                    [pick(side + k), pick(side + SPLIT + k) if SPLIT + k < CAP else none], axis=1
                )
                for k in range(SPLIT)
            ],
            axis=0,
        )
        found = jnp.dot(hot, rows, preferred_element_type=jnp.float32)
        value = found[:CX]
        for k in range(1, SPLIT):
            value = value + pltpu.roll(found[k * CX : (k + 1) * CX], B - SPAN * k, 1)
        sums.append(value)
    lane = lax.broadcasted_iota(jnp.int32, (CX, B), 1)
    from_before = lane < 0
    for start, width in SPANS:
        from_before |= (lane >= start) & (lane < start + width)
    beside = jnp.where(from_before, sums[0], sums[1])
    own = [total[:, f * B : (f + 1) * B] for f in range(F)]
    for f in range(F):
        flux[f] = own[f]
    own = [own[0], own[1], forcing * (own[2] + steric * own[3])]
    fields = []
    for (start, width), value in zip(SPANS, own):
        moved = pltpu.roll(beside, B - width - start, 1)
        outer = jnp.where((lane >= B - width) | (lane < width), moved, 0.0)
        fields.append(jnp.concatenate([value, outer], axis=1))
    for i, field in enumerate(fields):
        wide[i] = field
    odd = parity[0] == 1
    firsts = [field[:8] for field in fields] + [state[i, :8] for i in range(4)]
    lasts = [field[CX - 8 :] for field in fields] + [state[i, CX - 8 :] for i in range(4)]
    for i, (first, last) in enumerate(zip(firsts, lasts)):
        to_pair[i] = jnp.where(odd, first, last)
        to_beside[i] = jnp.where(odd, last, first)


def sum_rows(parity, arrived, state, devices):
    inside = pl.BlockSpec(memory_space=pltpu.VMEM)
    return pl.pallas_call(
        functools.partial(sum_kernel, devices=devices),
        out_shape=(
            jax.ShapeDtypeStruct((F, CX, B), jnp.float32),
            jax.ShapeDtypeStruct((3, CX, 2 * B), jnp.float32),
            jax.ShapeDtypeStruct((7, 8, 2 * B), jnp.float32),
            jax.ShapeDtypeStruct((7, 8, 2 * B), jnp.float32),
        ),
        in_specs=[pl.BlockSpec(memory_space=pltpu.SMEM), inside, inside],
        out_specs=(inside,) * 4,
        compiler_params=pltpu.CompilerParams(vmem_limit_bytes=32 << 20),
        name="sum_rows",
    )(parity, arrived, state)


def step_kernel(place, state, wide, pair, beside, height_out, zonal_out, merid_out):
    rows = CX + 16
    odd = place[0] == 1
    has_above = place[1] == 1
    has_below = place[2] == 1

    def field(i):
        above = jnp.where(odd, pair[i], beside[i])
        below = jnp.where(odd, beside[i], pair[i])
        own = wide[i] if i < 3 else state[i - 3]
        return jnp.concatenate(
            [jnp.where(has_above, above, 0.0), own, jnp.where(has_below, below, 0.0)], axis=0
        )

    zonal_flux, merid_flux, source = field(0), field(1), field(2)
    height, zonal, merid, depth = field(3), field(4), field(5), field(6)
    inside = depth > 0.0

    def grad_x(a):
        return 0.5 * (pltpu.roll(a, rows - 1, 0) - pltpu.roll(a, 1, 0))

    def grad_y(a):
        return 0.5 * (pltpu.roll(a, 2 * B - 1, 1) - pltpu.roll(a, 1, 1))

    for _ in range(STEPS):
        height = height - courant * depth * (grad_x(zonal) + grad_y(merid)) + source
        new_zonal = (
            zonal
            - courant * grad_x(height)
            + coriolis * merid
            + forcing * zonal_flux
            - damping * zonal
        )
        new_merid = (
            merid
            - courant * grad_y(height)
            - coriolis * zonal
            + forcing * merid_flux
            - damping * merid
        )
        zonal = jnp.where(inside, new_zonal, 0.0)
        merid = jnp.where(inside, new_merid, 0.0)
    height_out[...] = height[8 : 8 + CX, :B]
    zonal_out[...] = zonal[8 : 8 + CX, :B]
    merid_out[...] = merid[8 : 8 + CX, :B]


def substeps(place, state, wide, pair, beside):
    inside = pl.BlockSpec(memory_space=pltpu.VMEM)
    shape = jax.ShapeDtypeStruct((CX, B), jnp.float32)
    return pl.pallas_call(
        step_kernel,
        out_shape=(shape,) * 3,
        in_specs=[pl.BlockSpec(memory_space=pltpu.SMEM)] + [inside] * 4,
        out_specs=(inside,) * 3,
        compiler_params=pltpu.CompilerParams(vmem_limit_bytes=32 << 20),
        name="substeps",
    )(place, state, wide, pair, beside)


def around(x, axis, by):
    n = lax.axis_size(axis)
    return lax.ppermute(x, axis, [(i, (i + by) % n) for i in range(n)])


def on_device(
    source_flux,
    remap_weights,
    source_block,
    owner_device,
    target_row,
    sea_height,
    u_velocity,
    v_velocity,
    ocean_depth,
):
    ocn = lax.axis_size("ocn")
    devices = lax.axis_size("atm") * ocn
    messages = pack(
        owner_device[:, 0], target_row, source_block, source_flux, remap_weights, devices, ocn
    )
    arrived = lax.all_to_all(
        messages.reshape(-1, 1, B), AXES, split_axis=0, concat_axis=0, tiled=True
    ).reshape(-1, B)

    column = lax.axis_index("ocn")
    line = lax.axis_index("atm")
    lines = lax.axis_size("atm")
    place = jnp.stack([line % 2, line > 0, line < lines - 1]).astype(jnp.int32)
    state = jnp.stack([sea_height, u_velocity, v_velocity, ocean_depth])
    state, messages = lax.optimization_barrier((state, messages))
    before = around(state[:, :, B - REACH :], "ocn", 1)
    after = around(state[:, :, :REACH], "ocn", -1)
    before = jnp.where(column > 0, before, 0.0)
    after = jnp.where(column < ocn - 1, after, 0.0)
    gap = jnp.zeros((4, CX, B - 2 * REACH), jnp.float32)
    state = jnp.concatenate([state, after, gap, before], axis=2)

    flux, wide, to_pair, to_beside = sum_rows(place[:1], arrived, state, devices)
    pair = lax.ppermute(to_pair, "atm", [(i, i ^ 1) for i in range(lines)])
    beside = lax.ppermute(
        to_beside, "atm", [(i, (i + 1 if i % 2 else i - 1) % lines) for i in range(lines)]
    )
    height, zonal, merid = substeps(place, state, wide, pair, beside)
    return flux, height, zonal, merid


def solution(mesh):
    placed = (
        P(None, AXES),
        P(AXES, None, None),
        P(AXES),
        P(AXES, None),
        P(AXES),
        P("atm", "ocn"),
        P("atm", "ocn"),
        P("atm", "ocn"),
        P("atm", "ocn"),
    )
    return jax.shard_map(
        on_device,
        mesh=mesh,
        in_specs=placed,
        out_specs=(P(None, "atm", "ocn"), P("atm", "ocn"), P("atm", "ocn"), P("atm", "ocn")),
        check_vma=False,
    )
```

time: 78.6 us -> 67.2 us (0.85)
  the two profiles are of different devices: /device:TPU:59 before, /device:TPU:0 now
where the time goes in v2:
time: 67.2 us; the launch traced here: 67 us
  waiting for transfers between devices  34.2 us (51%)
  starting transfers between devices  17.9 us (27%)
  Pallas kernels  12.4 us (18%)
  other arithmetic  1.5 us (2%)
  between operations  0.76 us (1%)
    ppermute x2, waiting for transfers between devices, around(): return lax.ppermute(x, axis, [(i, (i + by) % n) for i in range(n)])  28.3 us
    all_to_all x1, starting transfers between devices, on_device(): lax.all_to_all(messages.reshape(-1, 1, B), AXES, split_axis=0, concat_axi...  11.2 us
    pallas_call x1, Pallas kernels, pack(): pl.pallas_call(functools.partial(pack_kernel, devices=devices, ocn=ocn),...  9.32 us
    ppermute x1, waiting for transfers between devices, on_device(): lax.ppermute(to_beside, 'atm', [(i, (i + 1 if i % 2 else i - 1) % lines)...  3.55 us
    ppermute x2, starting transfers between devices, around(): return lax.ppermute(x, axis, [(i, (i + by) % n) for i in range(n)])  3.31 us
    ppermute x1, starting transfers between devices, on_device(): lax.ppermute(to_beside, 'atm', [(i, (i + 1 if i % 2 else i - 1) % lines)...  3.29 us
    all_to_all x1, waiting for transfers between devices, on_device(): lax.all_to_all(messages.reshape(-1, 1, B), AXES, split_axis=0, concat_axi...  2.41 us
    pallas_call x1, Pallas kernels, substeps(): pl.pallas_call(step_kernel, out_shape=(shape,) * 3, in_specs=[pl.BlockSpe...  1.82 us
  transfers between devices with their start and end apart: 5, of which 3 were waited for; matrix products, arithmetic and copies ran while one was open for 1% of the time, Pallas kernels for 0%

profile of v2, /device:TPU:0, one launch (start us, length us, event | category | flops | bytes accessed | tf_op | source)
XLA Modules:
  0.0 67.0 jit_solution(15505690035836084263)
XLA Ops:
  0.6 1.3 %reduce.owner_h = s32[576]{0:T(1024)} reduce(s32[576,1]{0,1:T(1,128)} %param.12, s32[]{:T(128)} %constant.23.clone.1), dimensions={1}, to_apply=%param.12.reduce_sub_computation | reduce | bytes 4612 | tf_op args[3]
  1.9 9.3 %remap_pack.1 = f32[4864,128]{1,0:T(8,128)} custom-call(s32[576]{0:T(1024)} %reduce.owner_h, s32[576]{0:T(1024)} %target_h.1, s32[576]{0:T(1024)} %block_h.1, bf16[4,2048]{1,0:T(4,128)(2,1)} %src_h.1, bf16[576,128,128]{2,1,0:T(8,128)(2,1)} %weights_h.1), custom_call_target="tpu_custom_call" | custom-call | flops 75497472 | bytes 18874368 | tf_op jit(solution)/shard_map/remap_pack/pallas_call | solution.py:150
  11.2 0.0 copy-start
  11.3 0.0 copy-start.1
  11.3 0.0 copy-start.2
  11.3 0.0 copy-start.3
  11.3 11.2 %all-to-all-start = ((f32[4864,1,128]{2,1,0:T(1,128)}), f32[4864,1,128]{2,1,0:T(1,128)S(1)}, u32[]{:S(2)}, u32[]{:S(2)}) async-start(f32[4864,1,128]{2,1,0:T(1,128)} %bitcast.12), calls=%async_computation | async-start | bytes 4980736 | tf_op jit(solution)/shard_map/all_to_all | solution.py:344
  22.5 0.0 copy-done
  22.5 0.0 copy-done.1
  22.5 0.0 copy-done.2
  22.5 0.0 copy-done.3
  22.5 0.1 fusion
  22.6 1.1 %collective-permute-start.1 = (f32[4,64,6]{2,1,0:T(8,128)S(1)}, f32[4,64,6]{2,1,0:T(8,128)S(1)}, u32[]{:S(2)}, u32[]{:S(2)}) collective-permute-start(f32[4,64,6]{2,1,0:T(8,128)S(1)} %get-tuple-element.21), channel_id=1, source_target_pairs={{0,1},{1,2},{2,3},{3,0},{4,5},{5,6},{6,7},{7,4},{8,9},{9,10},{10,1... | collective-permute-start | bytes 18440 | tf_op jit(solution)/shard_map/ppermute | solution.py:325
  23.8 2.2 %collective-permute-start = (f32[4,64,6]{2,1,0:T(8,128)S(1)}, f32[4,64,6]{2,1,0:T(8,128)S(1)}, u32[]{:S(2)}, u32[]{:S(2)}) collective-permute-start(f32[4,64,6]{2,1,0:T(8,128)S(1)} %get-tuple-element.20), channel_id=1, source_target_pairs={{0,3},{1,0},{2,1},{3,2},{4,7},{5,4},{6,5},{7,6},{8,11},{9,8},{10,9... | collective-permute-start | bytes 18440 | tf_op jit(solution)/shard_map/ppermute | solution.py:325
  25.9 0.1 pad.5.clone
  26.0 28.3 %collective-permute-done.1 = f32[4,64,6]{2,1,0:T(8,128)S(1)} collective-permute-done((f32[4,64,6]{2,1,0:T(8,128)S(1)}, f32[4,64,6]{2,1,0:T(8,128)S(1)}, u32[]{:S(2)}, u32[]{:S(2)}) %collective-permute-start.1) | collective-permute-done | bytes 6176 | tf_op jit(solution)/shard_map/ppermute | solution.py:325
  54.3 0.0 collective-permute-done
  54.3 0.1 pad_maximum_fusion.state
  54.4 2.4 %all-to-all-done = f32[4864,1,128]{2,1,0:T(1,128)S(1)} async-done(((f32[4864,1,128]{2,1,0:T(1,128)}), f32[4864,1,128]{2,1,0:T(1,128)S(1)}, u32[]{:S(2)}, u32[]{:S(2)}) %all-to-all-start) | async-done | bytes 2490400 | tf_op jit(solution)/shard_map/all_to_all | solution.py:344
  56.8 1.3 %sum_rows.1 = (f32[4,64,128]{2,1,0:T(8,128)}, f32[3,64,256]{2,1,0:T(8,128)S(1)}, f32[7,8,256]{2,1,0:T(8,128)S(1)}, f32[7,8,256]{2,1,0:T(8,128)S(1)}) custom-call(s32[1]{0:T(128)} %bitcast.parity, f32[4864,128]{1,0:T(8,128)S(1)} %bitcast.11, f32[4,64,256]{2,1,0:T(8,128)S(1)} %pad_maximum_fusion.state), custom_call_target="tpu_custom_call" | custom-call | tf_op jit(solution)/shard_map/sum_rows/pallas_call | solution.py:248
  58.1 0.1 collective-permute-start.2
  58.2 3.3 %collective-permute-start.3 = (f32[7,8,256]{2,1,0:T(8,128)S(1)}, f32[7,8,256]{2,1,0:T(8,128)S(1)}, u32[]{:S(2)}, u32[]{:S(2)}) collective-permute-start(f32[7,8,256]{2,1,0:T(8,128)S(1)} %get-tuple-element.16), channel_id=1, source_target_pairs={{0,124},{4,8},{8,4},{12,16},{16,12},{20,24},{24,20},{28,32},{32,28... | collective-permute-start | bytes 172040 | tf_op jit(solution)/shard_map/ppermute | solution.py:363
  61.5 0.1 pad_add_fusion.place
  61.6 0.0 collective-permute-done.2.pair
  61.6 3.6 %collective-permute-done.3.beside = f32[7,8,256]{2,1,0:T(8,128)S(1)} collective-permute-done((f32[7,8,256]{2,1,0:T(8,128)S(1)}, f32[7,8,256]{2,1,0:T(8,128)S(1)}, u32[]{:S(2)}, u32[]{:S(2)}) %collective-permute-start.3) | collective-permute-done | bytes 57376 | tf_op jit(solution)/shard_map/ppermute | solution.py:363
  65.1 1.8 %substeps.1 = (f32[64,128]{1,0:T(8,128)}, f32[64,128]{1,0:T(8,128)}, f32[64,128]{1,0:T(8,128)}) custom-call(s32[3]{0:T(128)S(1)} %pad_add_fusion.place, f32[4,64,256]{2,1,0:T(8,128)S(1)} %pad_maximum_fusion.state, f32[3,64,256]{2,1,0:T(8,128)S(1)} %get-tuple-element.14.wide, f32[7,8,256]{2,1,0:T(8,128)S(1)} %collective-permute-done.2.pair, ...), custom_call_target="tpu_custom_call" | custom-call | tf_op jit(solution)/shard_map/substeps/pallas_call | solution.py:313
  (4 shorter events, 0.0 us)
Async XLA Ops:
  11.2 11.2 %copy-start = (f32[64,128]{1,0:T(8,128)S(1)}, f32[64,128]{1,0:T(8,128)}, u32[]{:S(2)}) copy-start(f32[64,128]{1,0:T(8,128)} %param.17) | copy-start | bytes 98308
  11.3 11.2 %copy-start.1 = (f32[64,128]{1,0:T(8,128)S(1)}, f32[64,128]{1,0:T(8,128)}, u32[]{:S(2)}) copy-start(f32[64,128]{1,0:T(8,128)} %param.16) | copy-start | bytes 98308
  11.3 11.2 %copy-start.2 = (f32[64,128]{1,0:T(8,128)S(1)}, f32[64,128]{1,0:T(8,128)}, u32[]{:S(2)}) copy-start(f32[64,128]{1,0:T(8,128)} %param.15) | copy-start | bytes 98308
  11.3 11.2 %copy-start.3 = (f32[64,128]{1,0:T(8,128)S(1)}, f32[64,128]{1,0:T(8,128)}, u32[]{:S(2)}) copy-start(f32[64,128]{1,0:T(8,128)} %param.14) | copy-start | bytes 98308
  11.3 45.5 %all-to-all-start = ((f32[4864,1,128]{2,1,0:T(1,128)}), f32[4864,1,128]{2,1,0:T(1,128)S(1)}, u32[]{:S(2)}, u32[]{:S(2)}) async-start(f32[4864,1,128]{2,1,0:T(1,128)} %bitcast.12), calls=%async_computation | async-start | bytes 4980736 | tf_op jit(solution)/shard_map/all_to_all | solution.py:344
  22.6 31.6 %collective-permute-start.1 = (f32[4,64,6]{2,1,0:T(8,128)S(1)}, f32[4,64,6]{2,1,0:T(8,128)S(1)}, u32[]{:S(2)}, u32[]{:S(2)}) collective-permute-start(f32[4,64,6]{2,1,0:T(8,128)S(1)} %get-tuple-element.21), channel_id=1, source_target_pairs={{0,1},{1,2},{2,3},{3,0},{4,5},{5,6},{6,7},{7,4},{8,9},{9,10},{10,1... | collective-permute-start | bytes 18440 | tf_op jit(solution)/shard_map/ppermute | solution.py:325
  23.8 30.5 %collective-permute-start = (f32[4,64,6]{2,1,0:T(8,128)S(1)}, f32[4,64,6]{2,1,0:T(8,128)S(1)}, u32[]{:S(2)}, u32[]{:S(2)}) collective-permute-start(f32[4,64,6]{2,1,0:T(8,128)S(1)} %get-tuple-element.20), channel_id=1, source_target_pairs={{0,3},{1,0},{2,1},{3,2},{4,7},{5,4},{6,5},{7,6},{8,11},{9,8},{10,9... | collective-permute-start | bytes 18440 | tf_op jit(solution)/shard_map/ppermute | solution.py:325
  58.1 3.5 %collective-permute-start.2 = (f32[7,8,256]{2,1,0:T(8,128)S(1)}, f32[7,8,256]{2,1,0:T(8,128)S(1)}, u32[]{:S(2)}, u32[]{:S(2)}) collective-permute-start(f32[7,8,256]{2,1,0:T(8,128)S(1)} %get-tuple-element.15), channel_id=1, source_target_pairs={{0,4},{4,0},{8,12},{12,8},{16,20},{20,16},{24,28},{28,24},{32,36},... | collective-permute-start | bytes 172040 | tf_op jit(solution)/shard_map/ppermute | solution.py:362
  58.2 6.9 %collective-permute-start.3 = (f32[7,8,256]{2,1,0:T(8,128)S(1)}, f32[7,8,256]{2,1,0:T(8,128)S(1)}, u32[]{:S(2)}, u32[]{:S(2)}) collective-permute-start(f32[7,8,256]{2,1,0:T(8,128)S(1)} %get-tuple-element.16), channel_id=1, source_target_pairs={{0,124},{4,8},{8,4},{12,16},{16,12},{20,24},{24,20},{28,32},{32,28... | collective-permute-start | bytes 172040 | tf_op jit(solution)/shard_map/ppermute | solution.py:363

commit v3 on v2

--- a/solution.py
+++ b/solution.py
@@ -19,6 +19,7 @@
 SPLIT = 5
 LABELS = 96
 CHUNKS = 16
+AHEAD = 2
 
 courant = 0.5
 forcing = 0.3
@@ -68,7 +69,8 @@
         )
         for c in range(CHUNKS)
     ]
-    copies[0].start()
+    for copy in copies[:AHEAD]:
+        copy.start()
     built[...] = jnp.zeros(built.shape, jnp.float32)
     labels[...] = jnp.full(labels.shape, -1.0, jnp.float32)
 
@@ -87,7 +89,7 @@
             lhs[j, b] = jnp.concatenate(parts, 0).astype(jnp.bfloat16)
     for copy in smalls[1:]:
         copy.wait()
-    for copy in copies[1:]:
+    for copy in copies[AHEAD:]:
         copy.start()
     lane = lax.broadcasted_iota(jnp.int32, (1, B), 1)
     for c in range(CHUNKS):
@@ -97,7 +99,7 @@
             right = weights[w : w + 4].reshape(4 * B, B)
             rows = jnp.dot(left, right, preferred_element_type=jnp.float32)
             for j in range(4):
-                o = owner[w + j]
+                o = owner[0, w + j]
                 k = count[o]
                 count[o] = k + 1
                 built[pl.ds(o * ROWS + k * F, F), :] = rows[F * j : F * (j + 1)]
@@ -157,7 +159,7 @@
             pltpu.VMEM((4, src.shape[1] // B, 4 * F, B), jnp.bfloat16),
             pltpu.VMEM((devices, B), jnp.float32),
             pltpu.VMEM(src.shape, jnp.bfloat16),
-            pltpu.SMEM((total,), jnp.int32),
+            pltpu.SMEM((1, total), jnp.int32),
             pltpu.SMEM((total,), jnp.int32),
             pltpu.SMEM((total,), jnp.int32),
             pltpu.SMEM((devices,), jnp.int32),
@@ -180,7 +182,7 @@
     return jnp.concatenate([high, low], axis=0)
 
 
-def sum_kernel(parity, arrived, state, flux, wide, to_pair, to_beside, *, devices):
+def sum_kernel(arrived, state, flux, wide, to_pair, to_beside, *, devices):
     names = arrived[pl.ds(37, devices, stride=ROWS), :].T
     row = lax.broadcasted_iota(jnp.int32, (CX, devices), 0).astype(jnp.float32)
 
@@ -235,7 +237,7 @@
         fields.append(jnp.concatenate([value, outer], axis=1))
     for i, field in enumerate(fields):
         wide[i] = field
-    odd = parity[0] == 1
+    odd = lax.axis_index("atm") % 2 == 1
     firsts = [field[:8] for field in fields] + [state[i, :8] for i in range(4)]
     lasts = [field[CX - 8 :] for field in fields] + [state[i, CX - 8 :] for i in range(4)]
     for i, (first, last) in enumerate(zip(firsts, lasts)):
@@ -243,7 +245,7 @@
         to_beside[i] = jnp.where(odd, last, first)
 
 
-def sum_rows(parity, arrived, state, devices):
+def sum_rows(arrived, state, devices):
     inside = pl.BlockSpec(memory_space=pltpu.VMEM)
     return pl.pallas_call(
         functools.partial(sum_kernel, devices=devices),
@@ -253,18 +255,23 @@
             jax.ShapeDtypeStruct((7, 8, 2 * B), jnp.float32),
             jax.ShapeDtypeStruct((7, 8, 2 * B), jnp.float32),
         ),
-        in_specs=[pl.BlockSpec(memory_space=pltpu.SMEM), inside, inside],
+        in_specs=[inside] * 2,
         out_specs=(inside,) * 4,
         compiler_params=pltpu.CompilerParams(vmem_limit_bytes=32 << 20),
         name="sum_rows",
-    )(parity, arrived, state)
-
-
-def step_kernel(place, state, wide, pair, beside, height_out, zonal_out, merid_out):
+    )(arrived, state)
+
+
+def step_kernel(
+    state, flux, wide, pair, beside, flux_out, height_out, zonal_out, merid_out, sem, *, lines
+):
+    send = pltpu.make_async_copy(flux, flux_out, sem)
+    send.start()
     rows = CX + 16
-    odd = place[0] == 1
-    has_above = place[1] == 1
-    has_below = place[2] == 1
+    line = lax.axis_index("atm")
+    odd = line % 2 == 1
+    has_above = line > 0
+    has_below = line < lines - 1
 
     def field(i):
         above = jnp.where(odd, pair[i], beside[i])
@@ -305,19 +312,21 @@
     height_out[...] = height[8 : 8 + CX, :B]
     zonal_out[...] = zonal[8 : 8 + CX, :B]
     merid_out[...] = merid[8 : 8 + CX, :B]
-
-
-def substeps(place, state, wide, pair, beside):
+    send.wait()
+
+
+def substeps(state, flux, wide, pair, beside, lines):
     inside = pl.BlockSpec(memory_space=pltpu.VMEM)
     shape = jax.ShapeDtypeStruct((CX, B), jnp.float32)
     return pl.pallas_call(
-        step_kernel,
-        out_shape=(shape,) * 3,
-        in_specs=[pl.BlockSpec(memory_space=pltpu.SMEM)] + [inside] * 4,
-        out_specs=(inside,) * 3,
+        functools.partial(step_kernel, lines=lines),
+        out_shape=(jax.ShapeDtypeStruct((F, CX, B), jnp.float32),) + (shape,) * 3,
+        in_specs=[inside] * 5,
+        out_specs=(pl.BlockSpec(memory_space=pltpu.HBM),) + (inside,) * 3,
+        scratch_shapes=[pltpu.SemaphoreType.DMA],
         compiler_params=pltpu.CompilerParams(vmem_limit_bytes=32 << 20),
         name="substeps",
-    )(place, state, wide, pair, beside)
+    )(state, flux, wide, pair, beside)
 
 
 def around(x, axis, by):
@@ -339,16 +348,14 @@
     ocn = lax.axis_size("ocn")
     devices = lax.axis_size("atm") * ocn
     messages = pack(
-        owner_device[:, 0], target_row, source_block, source_flux, remap_weights, devices, ocn
+        owner_device.T, target_row, source_block, source_flux, remap_weights, devices, ocn
     )
     arrived = lax.all_to_all(
         messages.reshape(-1, 1, B), AXES, split_axis=0, concat_axis=0, tiled=True
     ).reshape(-1, B)
 
     column = lax.axis_index("ocn")
-    line = lax.axis_index("atm")
     lines = lax.axis_size("atm")
-    place = jnp.stack([line % 2, line > 0, line < lines - 1]).astype(jnp.int32)
     state = jnp.stack([sea_height, u_velocity, v_velocity, ocean_depth])
     state, messages = lax.optimization_barrier((state, messages))
     before = around(state[:, :, B - REACH :], "ocn", 1)
@@ -358,13 +365,12 @@
     gap = jnp.zeros((4, CX, B - 2 * REACH), jnp.float32)
     state = jnp.concatenate([state, after, gap, before], axis=2)
 
-    flux, wide, to_pair, to_beside = sum_rows(place[:1], arrived, state, devices)
+    flux, wide, to_pair, to_beside = sum_rows(arrived, state, devices)
     pair = lax.ppermute(to_pair, "atm", [(i, i ^ 1) for i in range(lines)])
     beside = lax.ppermute(
         to_beside, "atm", [(i, (i + 1 if i % 2 else i - 1) % lines) for i in range(lines)]
     )
-    height, zonal, merid = substeps(place, state, wide, pair, beside)
-    return flux, height, zonal, merid
+    return substeps(state, flux, wide, pair, beside, lines)
 
 
 def solution(mesh):

time: 67.2 us -> 64.9 us (0.966)
  other arithmetic: 1.5 us -> 0.14 us
  Pallas kernels: 12.4 us -> 11.3 us
    unnamed x1 -> x0, other arithmetic: 1.29 us -> none
    ppermute x2, waiting for transfers between devices: 28.3 us -> 29.3 us  [around(): return lax.ppermute(x, axis, [(i, (i + by) % n) for i in range(n)])]
  transfers between devices with their start and end apart: 5 -> 5, of which waited for: 3 -> 4; matrix products, arithmetic and copies ran while one was open for 1% -> 0% of each run, Pallas kernels for 0% -> 0%
where the time goes in v3:
time: 64.9 us; the launch traced here: 64.7 us
  waiting for transfers between devices  34.8 us (54%)
  starting transfers between devices  17.5 us (27%)
  Pallas kernels  11.3 us (17%)
  between operations  0.75 us (1%)
    ppermute x2, waiting for transfers between devices, around(): return lax.ppermute(x, axis, [(i, (i + by) % n) for i in range(n)])  29.3 us
    all_to_all x1, starting transfers between devices, on_device(): lax.all_to_all(messages.reshape(-1, 1, B), AXES, split_axis=0, concat_axi...  11.1 us
    pallas_call x1, Pallas kernels, pack(): pl.pallas_call(functools.partial(pack_kernel, devices=devices, ocn=ocn),...  9.05 us
    ppermute x1, waiting for transfers between devices, on_device(): lax.ppermute(to_beside, 'atm', [(i, (i + 1 if i % 2 else i - 1) % lines)...  3.66 us
    ppermute x1, starting transfers between devices, on_device(): lax.ppermute(to_beside, 'atm', [(i, (i + 1 if i % 2 else i - 1) % lines)...  3.26 us
    ppermute x2, starting transfers between devices, around(): return lax.ppermute(x, axis, [(i, (i + by) % n) for i in range(n)])  2.9 us
    all_to_all x1, waiting for transfers between devices, on_device(): lax.all_to_all(messages.reshape(-1, 1, B), AXES, split_axis=0, concat_axi...  1.82 us
    pallas_call x1, Pallas kernels, substeps(): pl.pallas_call(functools.partial(step_kernel, lines=lines), out_shape=(ja...  1.31 us
  transfers between devices with their start and end apart: 5, of which 4 were waited for; matrix products, arithmetic and copies ran while one was open for 0% of the time, Pallas kernels for 0%

profile of v3, /device:TPU:0, one launch (start us, length us, event | category | flops | bytes accessed | tf_op | source)
XLA Modules:
  0.0 64.7 jit_solution(2605191718835074973)
XLA Ops:
  0.6 9.1 %remap_pack.1 = f32[4864,128]{1,0:T(8,128)} custom-call(s32[1,576]{1,0:T(1,128)} %bitcast.15, s32[576]{0:T(1024)} %target_h.1, s32[576]{0:T(1024)} %block_h.1, bf16[4,2048]{1,0:T(4,128)(2,1)} %src_h.1, bf16[576,128,128]{2,1,0:T(8,128)(2,1)} %weights_h.1), custom_call_target="tpu_custom_call" | custom-call | flops 75497472 | bytes 18874368 | tf_op jit(solution)/shard_map/remap_pack/pallas_call | solution.py:152
  9.7 0.0 copy-start
  9.7 0.0 copy-start.1
  9.7 0.0 copy-start.2
  9.7 0.0 copy-start.3
  9.7 11.1 %all-to-all-start = ((f32[4864,1,128]{2,1,0:T(1,128)}), f32[4864,1,128]{2,1,0:T(1,128)S(1)}, u32[]{:S(2)}, u32[]{:S(2)}) async-start(f32[4864,1,128]{2,1,0:T(1,128)} %bitcast.10), calls=%async_computation | async-start | bytes 4980736 | tf_op jit(solution)/shard_map/all_to_all | solution.py:353
  20.9 0.0 copy-done
  20.9 0.0 copy-done.1
  20.9 0.0 copy-done.2
  20.9 0.0 copy-done.3
  21.0 0.1 fusion
  21.1 2.9 %collective-permute-start = (f32[4,64,6]{2,1,0:T(8,128)S(1)}, f32[4,64,6]{2,1,0:T(8,128)S(1)}, u32[]{:S(2)}, u32[]{:S(2)}) collective-permute-start(f32[4,64,6]{2,1,0:T(8,128)S(1)} %get-tuple-element.14), channel_id=1, source_target_pairs={{0,3},{1,0},{2,1},{3,2},{4,7},{5,4},{6,5},{7,6},{8,11},{9,8},{10,9... | collective-permute-start | bytes 18440 | tf_op jit(solution)/shard_map/ppermute | solution.py:334
  24.0 0.0 collective-permute-start.1
  24.0 0.1 pad.2.clone
  24.0 27.4 %collective-permute-done = f32[4,64,6]{2,1,0:T(8,128)S(1)} collective-permute-done((f32[4,64,6]{2,1,0:T(8,128)S(1)}, f32[4,64,6]{2,1,0:T(8,128)S(1)}, u32[]{:S(2)}, u32[]{:S(2)}) %collective-permute-start) | collective-permute-done | bytes 6176 | tf_op jit(solution)/shard_map/ppermute | solution.py:334
  51.5 1.9 %collective-permute-done.1 = f32[4,64,6]{2,1,0:T(8,128)S(1)} collective-permute-done((f32[4,64,6]{2,1,0:T(8,128)S(1)}, f32[4,64,6]{2,1,0:T(8,128)S(1)}, u32[]{:S(2)}, u32[]{:S(2)}) %collective-permute-start.1) | collective-permute-done | bytes 6176 | tf_op jit(solution)/shard_map/ppermute | solution.py:334
  53.3 0.1 pad_maximum_fusion.state
  53.4 1.8 %all-to-all-done = f32[4864,1,128]{2,1,0:T(1,128)S(1)} async-done(((f32[4864,1,128]{2,1,0:T(1,128)}), f32[4864,1,128]{2,1,0:T(1,128)S(1)}, u32[]{:S(2)}, u32[]{:S(2)}) %all-to-all-start) | async-done | bytes 2490400 | tf_op jit(solution)/shard_map/all_to_all | solution.py:353
  55.3 1.0 %sum_rows.1 = (f32[4,64,128]{2,1,0:T(8,128)S(1)}, f32[3,64,256]{2,1,0:T(8,128)S(1)}, f32[7,8,256]{2,1,0:T(8,128)S(1)}, f32[7,8,256]{2,1,0:T(8,128)S(1)}) custom-call(f32[4864,128]{1,0:T(8,128)S(1)} %bitcast.9, f32[4,64,256]{2,1,0:T(8,128)S(1)} %pad_maximum_fusion.state), custom_call_target="tpu_custom_call" | custom-call | tf_op jit(solution)/shard_map/sum_rows/pallas_call | solution.py:250
  56.3 0.2 collective-permute-start.2
  56.5 3.3 %collective-permute-start.3 = (f32[7,8,256]{2,1,0:T(8,128)S(1)}, f32[7,8,256]{2,1,0:T(8,128)S(1)}, u32[]{:S(2)}, u32[]{:S(2)}) collective-permute-start(f32[7,8,256]{2,1,0:T(8,128)S(1)} %get-tuple-element.13), channel_id=1, source_target_pairs={{0,124},{4,8},{8,4},{12,16},{16,12},{20,24},{24,20},{28,32},{32,28... | collective-permute-start | bytes 172040 | tf_op jit(solution)/shard_map/ppermute | solution.py:370
  59.7 0.0 collective-permute-done.2.pair
  59.7 3.7 %collective-permute-done.3.beside = f32[7,8,256]{2,1,0:T(8,128)S(1)} collective-permute-done((f32[7,8,256]{2,1,0:T(8,128)S(1)}, f32[7,8,256]{2,1,0:T(8,128)S(1)}, u32[]{:S(2)}, u32[]{:S(2)}) %collective-permute-start.3) | collective-permute-done | bytes 57376 | tf_op jit(solution)/shard_map/ppermute | solution.py:370
  63.4 1.3 %substeps.1 = (f32[4,64,128]{2,1,0:T(8,128)}, f32[64,128]{1,0:T(8,128)}, f32[64,128]{1,0:T(8,128)}, f32[64,128]{1,0:T(8,128)}) custom-call(f32[4,64,256]{2,1,0:T(8,128)S(1)} %pad_maximum_fusion.state, f32[4,64,128]{2,1,0:T(8,128)S(1)} %get-tuple-element.10.flux, f32[3,64,256]{2,1,0:T(8,128)S(1)} %get-tuple-element.11.wide, ...), custom_call_target="tpu_custom_call" | custom-call | tf_op jit(solution)/shard_map/substeps/pallas_call | solution.py:321
  (4 shorter events, 0.0 us)
Async XLA Ops:
  9.7 11.2 %copy-start = (f32[64,128]{1,0:T(8,128)S(1)}, f32[64,128]{1,0:T(8,128)}, u32[]{:S(2)}) copy-start(f32[64,128]{1,0:T(8,128)} %param.17) | copy-start | bytes 98308
  9.7 11.2 %copy-start.1 = (f32[64,128]{1,0:T(8,128)S(1)}, f32[64,128]{1,0:T(8,128)}, u32[]{:S(2)}) copy-start(f32[64,128]{1,0:T(8,128)} %param.16) | copy-start | bytes 98308
  9.7 11.2 %copy-start.2 = (f32[64,128]{1,0:T(8,128)S(1)}, f32[64,128]{1,0:T(8,128)}, u32[]{:S(2)}) copy-start(f32[64,128]{1,0:T(8,128)} %param.15) | copy-start | bytes 98308
  9.7 11.2 %copy-start.3 = (f32[64,128]{1,0:T(8,128)S(1)}, f32[64,128]{1,0:T(8,128)}, u32[]{:S(2)}) copy-start(f32[64,128]{1,0:T(8,128)} %param.14) | copy-start | bytes 98308
  9.7 45.5 %all-to-all-start = ((f32[4864,1,128]{2,1,0:T(1,128)}), f32[4864,1,128]{2,1,0:T(1,128)S(1)}, u32[]{:S(2)}, u32[]{:S(2)}) async-start(f32[4864,1,128]{2,1,0:T(1,128)} %bitcast.10), calls=%async_computation | async-start | bytes 4980736 | tf_op jit(solution)/shard_map/all_to_all | solution.py:353
  21.1 30.4 %collective-permute-start = (f32[4,64,6]{2,1,0:T(8,128)S(1)}, f32[4,64,6]{2,1,0:T(8,128)S(1)}, u32[]{:S(2)}, u32[]{:S(2)}) collective-permute-start(f32[4,64,6]{2,1,0:T(8,128)S(1)} %get-tuple-element.14), channel_id=1, source_target_pairs={{0,3},{1,0},{2,1},{3,2},{4,7},{5,4},{6,5},{7,6},{8,11},{9,8},{10,9... | collective-permute-start | bytes 18440 | tf_op jit(solution)/shard_map/ppermute | solution.py:334
  24.0 29.4 %collective-permute-start.1 = (f32[4,64,6]{2,1,0:T(8,128)S(1)}, f32[4,64,6]{2,1,0:T(8,128)S(1)}, u32[]{:S(2)}, u32[]{:S(2)}) collective-permute-start(f32[4,64,6]{2,1,0:T(8,128)S(1)} %get-tuple-element.15), channel_id=1, source_target_pairs={{0,1},{1,2},{2,3},{3,0},{4,5},{5,6},{6,7},{7,4},{8,9},{9,10},{10,1... | collective-permute-start | bytes 18440 | tf_op jit(solution)/shard_map/ppermute | solution.py:334
  56.3 3.5 %collective-permute-start.2 = (f32[7,8,256]{2,1,0:T(8,128)S(1)}, f32[7,8,256]{2,1,0:T(8,128)S(1)}, u32[]{:S(2)}, u32[]{:S(2)}) collective-permute-start(f32[7,8,256]{2,1,0:T(8,128)S(1)} %get-tuple-element.12), channel_id=1, source_target_pairs={{0,4},{4,0},{8,12},{12,8},{16,20},{20,16},{24,28},{28,24},{32,36},... | collective-permute-start | bytes 172040 | tf_op jit(solution)/shard_map/ppermute | solution.py:369
  56.5 6.9 %collective-permute-start.3 = (f32[7,8,256]{2,1,0:T(8,128)S(1)}, f32[7,8,256]{2,1,0:T(8,128)S(1)}, u32[]{:S(2)}, u32[]{:S(2)}) collective-permute-start(f32[7,8,256]{2,1,0:T(8,128)S(1)} %get-tuple-element.13), channel_id=1, source_target_pairs={{0,124},{4,8},{8,4},{12,16},{16,12},{20,24},{24,20},{28,32},{32,28... | collective-permute-start | bytes 172040 | tf_op jit(solution)/shard_map/ppermute | solution.py:370

commit v4 on v3

--- a/solution.py
+++ b/solution.py
@@ -18,8 +18,8 @@
 SPAN = 24
 SPLIT = 5
 LABELS = 96
-CHUNKS = 16
-AHEAD = 2
+CHUNKS = 24
+GROUP = 4
 
 courant = 0.5
 forcing = 0.3
@@ -62,15 +62,15 @@
         )
     ]
     for copy in smalls:
-        copy.start()
+        copy.start(priority=0)
     copies = [
         pltpu.make_async_copy(
             weights_h.at[pl.ds(c * per, per)], weights.at[pl.ds(c * per, per)], sems.at[c]
         )
         for c in range(CHUNKS)
     ]
-    for copy in copies[:AHEAD]:
-        copy.start()
+    for copy in copies:
+        copy.start(priority=1)
     built[...] = jnp.zeros(built.shape, jnp.float32)
     labels[...] = jnp.full(labels.shape, -1.0, jnp.float32)
 
@@ -89,8 +89,6 @@
             lhs[j, b] = jnp.concatenate(parts, 0).astype(jnp.bfloat16)
     for copy in smalls[1:]:
         copy.wait()
-    for copy in copies[AHEAD:]:
-        copy.start()
     lane = lax.broadcasted_iota(jnp.int32, (1, B), 1)
     for c in range(CHUNKS):
         copies[c].wait()
@@ -103,11 +101,10 @@
                 k = count[o]
                 count[o] = k + 1
                 built[pl.ds(o * ROWS + k * F, F), :] = rows[F * j : F * (j + 1)]
-                labels[pl.ds(o, 1), :] = jnp.where(
-                    lane == k, target[w + j].astype(jnp.float32), labels[pl.ds(o, 1), :]
-                )
-
-    group = 8 * ocn
+                name = jnp.full((1, B), target[w + j].astype(jnp.float32))
+                pltpu.store(labels.at[pl.ds(o, 1), :], name, mask=lane == k)
+
+    group = GROUP * ocn
     lane = lax.broadcasted_iota(jnp.int32, (group, B), 1)
     place = lax.broadcasted_iota(jnp.int32, (group, B), 0) % ocn
     sends = []
@@ -166,7 +163,7 @@
             pltpu.VMEM((devices * ROWS, B), jnp.float32),
             pltpu.SemaphoreType.DMA((CHUNKS,)),
             pltpu.SemaphoreType.DMA((4,)),
-            pltpu.SemaphoreType.DMA((devices // (8 * ocn),)),
+            pltpu.SemaphoreType.DMA((devices // (GROUP * ocn),)),
         ],
         compiler_params=pltpu.CompilerParams(vmem_limit_bytes=60 << 20),
         cost_estimate=pl.CostEstimate(
@@ -238,11 +235,17 @@
     for i, field in enumerate(fields):
         wide[i] = field
     odd = lax.axis_index("atm") % 2 == 1
-    firsts = [field[:8] for field in fields] + [state[i, :8] for i in range(4)]
-    lasts = [field[CX - 8 :] for field in fields] + [state[i, CX - 8 :] for i in range(4)]
-    for i, (first, last) in enumerate(zip(firsts, lasts)):
-        to_pair[i] = jnp.where(odd, first, last)
-        to_beside[i] = jnp.where(odd, last, first)
+    outers = [field[:, B:] for field in fields] + [state[i, :, B:] for i in range(4)]
+    top, bottom = slice(0, 8), slice(CX - 8, CX)
+    for rows, other, message in ((top, bottom, to_pair), (bottom, top, to_beside)):
+        packed = jnp.zeros((8, B), jnp.float32)
+        for i, outer in enumerate(outers):
+            at = 2 * REACH * i
+            moved = pltpu.roll(jnp.where(odd, outer[rows], outer[other]), at + REACH, 1)
+            packed = jnp.where((lane[:8] >= at) & (lane[:8] < at + 2 * REACH), moved, packed)
+        for i, field in enumerate(fields):
+            message[i] = jnp.where(odd, field[rows, :B], field[other, :B])
+        message[3] = packed
 
 
 def sum_rows(arrived, state, devices):
@@ -252,8 +255,8 @@
         out_shape=(
             jax.ShapeDtypeStruct((F, CX, B), jnp.float32),
             jax.ShapeDtypeStruct((3, CX, 2 * B), jnp.float32),
-            jax.ShapeDtypeStruct((7, 8, 2 * B), jnp.float32),
-            jax.ShapeDtypeStruct((7, 8, 2 * B), jnp.float32),
+            jax.ShapeDtypeStruct((4, 8, B), jnp.float32),
+            jax.ShapeDtypeStruct((4, 8, B), jnp.float32),
         ),
         in_specs=[inside] * 2,
         out_specs=(inside,) * 4,
@@ -263,7 +266,20 @@
 
 
 def step_kernel(
-    state, flux, wide, pair, beside, flux_out, height_out, zonal_out, merid_out, sem, *, lines
+    state,
+    flux,
+    wide,
+    pair,
+    beside,
+    state_pair,
+    state_beside,
+    flux_out,
+    height_out,
+    zonal_out,
+    merid_out,
+    sem,
+    *,
+    lines,
 ):
     send = pltpu.make_async_copy(flux, flux_out, sem)
     send.start()
@@ -273,12 +289,28 @@
     has_above = line > 0
     has_below = line < lines - 1
 
+    lane = lax.broadcasted_iota(jnp.int32, (8, B), 1)
+    ends = (lane >= B - REACH) | (lane < REACH)
+
+    def chosen(i, by_pair, by_beside, valid):
+        return jnp.where(valid, jnp.where(odd, by_pair[i], by_beside[i]), 0.0)
+
+    above = [chosen(i, pair, beside, has_above) for i in range(4)]
+    below = [chosen(i, beside, pair, has_below) for i in range(4)]
+    above = above[:3] + [chosen(i, state_pair, state_beside, has_above) for i in range(4)] + above[3:]
+    below = below[:3] + [chosen(i, state_beside, state_pair, has_below) for i in range(4)] + below[3:]
+
     def field(i):
-        above = jnp.where(odd, pair[i], beside[i])
-        below = jnp.where(odd, beside[i], pair[i])
         own = wide[i] if i < 3 else state[i - 3]
+        by = (B - 2 * REACH * i - REACH) % B
         return jnp.concatenate(
-            [jnp.where(has_above, above, 0.0), own, jnp.where(has_below, below, 0.0)], axis=0
+            [
+                jnp.concatenate([rows[i], jnp.where(ends, pltpu.roll(rows[7], by, 1), 0.0)], axis=1)
+                if n != 1
+                else own
+                for n, rows in enumerate((above, None, below))
+            ],
+            axis=0,
         )
 
     zonal_flux, merid_flux, source = field(0), field(1), field(2)
@@ -291,21 +323,28 @@
     def grad_y(a):
         return 0.5 * (pltpu.roll(a, 2 * B - 1, 1) - pltpu.roll(a, 1, 1))
 
+    slope = (0.5 * courant) * depth
+    zonal_gain, merid_gain = forcing * zonal_flux, forcing * merid_flux
+
+    def diff_x(a):
+        return pltpu.roll(a, rows - 1, 0) - pltpu.roll(a, 1, 0)
+
+    def diff_y(a):
+        return pltpu.roll(a, 2 * B - 1, 1) - pltpu.roll(a, 1, 1)
+
     for _ in range(STEPS):
-        height = height - courant * depth * (grad_x(zonal) + grad_y(merid)) + source
+        height = height - slope * (diff_x(zonal) + diff_y(merid)) + source
         new_zonal = (
-            zonal
-            - courant * grad_x(height)
+            (1.0 - damping) * zonal
+            - (0.5 * courant) * diff_x(height)
             + coriolis * merid
-            + forcing * zonal_flux
-            - damping * zonal
+            + zonal_gain
         )
         new_merid = (
-            merid
-            - courant * grad_y(height)
+            (1.0 - damping) * merid
+            - (0.5 * courant) * diff_y(height)
             - coriolis * zonal
-            + forcing * merid_flux
-            - damping * merid
+            + merid_gain
         )
         zonal = jnp.where(inside, new_zonal, 0.0)
         merid = jnp.where(inside, new_merid, 0.0)
@@ -315,23 +354,40 @@
     send.wait()
 
 
-def substeps(state, flux, wide, pair, beside, lines):
+def substeps(lines, *args):
     inside = pl.BlockSpec(memory_space=pltpu.VMEM)
     shape = jax.ShapeDtypeStruct((CX, B), jnp.float32)
     return pl.pallas_call(
         functools.partial(step_kernel, lines=lines),
         out_shape=(jax.ShapeDtypeStruct((F, CX, B), jnp.float32),) + (shape,) * 3,
-        in_specs=[inside] * 5,
+        in_specs=[inside] * 7,
         out_specs=(pl.BlockSpec(memory_space=pltpu.HBM),) + (inside,) * 3,
         scratch_shapes=[pltpu.SemaphoreType.DMA],
         compiler_params=pltpu.CompilerParams(vmem_limit_bytes=32 << 20),
         name="substeps",
-    )(state, flux, wide, pair, beside)
+    )(*args)
 
 
 def around(x, axis, by):
     n = lax.axis_size(axis)
     return lax.ppermute(x, axis, [(i, (i + by) % n) for i in range(n)])
+
+
+def with_pair(x):
+    return lax.ppermute(x, "atm", [(i, i ^ 1) for i in range(lax.axis_size("atm"))])
+
+
+def with_beside(x):
+    lines, columns = lax.axis_size("atm"), lax.axis_size("ocn")
+    partners = []
+    for i in range(lines):
+        other = i + 1 if i % 2 else i - 1
+        for j in range(columns):
+            here = i * columns + j
+            partners.append(
+                (here, other * columns + j if 0 <= other < lines else here - j + (j ^ 1))
+            )
+    return lax.ppermute(x, AXES, partners)
 
 
 def on_device(
@@ -358,6 +414,10 @@
     lines = lax.axis_size("atm")
     state = jnp.stack([sea_height, u_velocity, v_velocity, ocean_depth])
     state, messages = lax.optimization_barrier((state, messages))
+    odd = lax.axis_index("atm") % 2 == 1
+    firsts, lasts = state[:, :8], state[:, CX - 8 :]
+    state_pair = with_pair(jnp.where(odd, firsts, lasts))
+    state_beside = with_beside(jnp.where(odd, lasts, firsts))
     before = around(state[:, :, B - REACH :], "ocn", 1)
     after = around(state[:, :, :REACH], "ocn", -1)
     before = jnp.where(column > 0, before, 0.0)
@@ -366,11 +426,9 @@
     state = jnp.concatenate([state, after, gap, before], axis=2)
 
     flux, wide, to_pair, to_beside = sum_rows(arrived, state, devices)
-    pair = lax.ppermute(to_pair, "atm", [(i, i ^ 1) for i in range(lines)])
-    beside = lax.ppermute(
-        to_beside, "atm", [(i, (i + 1 if i % 2 else i - 1) % lines) for i in range(lines)]
-    )
-    return substeps(state, flux, wide, pair, beside, lines)
+    pair = with_pair(to_pair)
+    beside = with_beside(to_beside)
+    return substeps(lines, state, flux, wide, pair, beside, state_pair, state_beside)
 
 
 def solution(mesh):

time: 64.9 us -> 62.4 us (0.961)
  the two profiles are of different devices: /device:TPU:0 before, /device:TPU:4 now
where the time goes in v4:
time: 62.4 us; the launch traced here: 61.2 us
  waiting for transfers between devices  29.9 us (48%)
  starting transfers between devices  19.1 us (31%)
  Pallas kernels  11 us (18%)
  between operations  0.77 us (1%)
    ppermute x2, waiting for transfers between devices, around(): return lax.ppermute(x, axis, [(i, (i + by) % n) for i in range(n)])  27.3 us
    all_to_all x1, starting transfers between devices, on_device(): lax.all_to_all(messages.reshape(-1, 1, B), AXES, split_axis=0, concat_axi...  10.5 us
    pallas_call x1, Pallas kernels, pack(): pl.pallas_call(functools.partial(pack_kernel, devices=devices, ocn=ocn),...  8.66 us
    ppermute x2, starting transfers between devices, with_beside(): return lax.ppermute(x, AXES, partners)  5 us
    ppermute x2, starting transfers between devices, around(): return lax.ppermute(x, axis, [(i, (i + by) % n) for i in range(n)])  3.44 us
    ppermute x2, waiting for transfers between devices, with_beside(): return lax.ppermute(x, AXES, partners)  2.6 us
    pallas_call x1, Pallas kernels, substeps(): pl.pallas_call(functools.partial(step_kernel, lines=lines), out_shape=(ja...  1.32 us
  transfers between devices with their start and end apart: 7, of which 3 were waited for; matrix products, arithmetic and copies ran while one was open for 1% of the time, Pallas kernels for 2%

profile of v4, /device:TPU:4, one launch (start us, length us, event | category | flops | bytes accessed | tf_op | source)
XLA Modules:
  0.0 61.2 jit_solution(2293098046107588132)
XLA Ops:
  0.6 8.7 %remap_pack.1 = f32[4864,128]{1,0:T(8,128)} custom-call(s32[1,576]{1,0:T(1,128)} %bitcast.15, s32[576]{0:T(1024)} %target_h.1, s32[576]{0:T(1024)} %block_h.1, bf16[4,2048]{1,0:T(4,128)(2,1)} %src_h.1, bf16[576,128,128]{2,1,0:T(8,128)(2,1)} %weights_h.1), custom_call_target="tpu_custom_call" | custom-call | flops 75497472 | bytes 18874368 | tf_op jit(solution)/shard_map/remap_pack/pallas_call | solution.py:149
  9.3 0.0 copy-start
  9.3 0.0 copy-start.1
  9.3 0.0 copy-start.2
  9.3 0.0 copy-start.3
  9.3 10.5 %all-to-all-start = ((f32[4864,1,128]{2,1,0:T(1,128)}), f32[4864,1,128]{2,1,0:T(1,128)S(1)}, u32[]{:S(2)}, u32[]{:S(2)}) async-start(f32[4864,1,128]{2,1,0:T(1,128)} %bitcast.10), calls=%async_computation | async-start | bytes 4980736 | tf_op jit(solution)/shard_map/all_to_all | solution.py:409
  19.9 0.0 copy-done
  19.9 0.0 copy-done.1
  19.9 0.0 copy-done.2
  19.9 0.0 copy-done.3
  19.9 0.1 fusion
  20.0 3.4 %collective-permute-start = (f32[4,64,6]{2,1,0:T(8,128)S(1)}, f32[4,64,6]{2,1,0:T(8,128)S(1)}, u32[]{:S(2)}, u32[]{:S(2)}) collective-permute-start(f32[4,64,6]{2,1,0:T(8,128)S(1)} %get-tuple-element.16), channel_id=1, source_target_pairs={{0,3},{1,0},{2,1},{3,2},{4,7},{5,4},{6,5},{7,6},{8,11},{9,8},{10,9... | collective-permute-start | bytes 18440 | tf_op jit(solution)/shard_map/ppermute | solution.py:373
  23.5 2.3 %collective-permute-start.5 = (f32[4,8,128]{2,1,0:T(8,128)S(1)}, f32[4,8,128]{2,1,0:T(8,128)S(1)}, u32[]{:S(2)}, u32[]{:S(2)}) collective-permute-start(f32[4,8,128]{2,1,0:T(8,128)S(1)} %get-tuple-element.14), channel_id=1, source_target_pairs={{0,1},{1,0},{2,3},{3,2},{4,8},{5,9},{6,10},{7,11},{8,4},{9,5},{10,... | collective-permute-start | bytes 49160 | tf_op jit(solution)/shard_map/ppermute | solution.py:390
  25.8 0.0 collective-permute-start.4
  25.8 0.0 collective-permute-start.1
  25.8 0.1 pad.2.clone
  25.9 25.6 %collective-permute-done = f32[4,64,6]{2,1,0:T(8,128)S(1)} collective-permute-done((f32[4,64,6]{2,1,0:T(8,128)S(1)}, f32[4,64,6]{2,1,0:T(8,128)S(1)}, u32[]{:S(2)}, u32[]{:S(2)}) %collective-permute-start) | collective-permute-done | bytes 6176 | tf_op jit(solution)/shard_map/ppermute | solution.py:373
  51.5 1.7 %collective-permute-done.1 = f32[4,64,6]{2,1,0:T(8,128)S(1)} collective-permute-done((f32[4,64,6]{2,1,0:T(8,128)S(1)}, f32[4,64,6]{2,1,0:T(8,128)S(1)}, u32[]{:S(2)}, u32[]{:S(2)}) %collective-permute-start.1) | collective-permute-done | bytes 6176 | tf_op jit(solution)/shard_map/ppermute | solution.py:373
  53.2 0.1 pad_maximum_fusion.state
  53.3 0.0 all-to-all-done
  53.4 1.0 %sum_rows.1 = (f32[4,64,128]{2,1,0:T(8,128)S(1)}, f32[3,64,256]{2,1,0:T(8,128)S(1)}, f32[4,8,128]{2,1,0:T(8,128)S(1)}, f32[4,8,128]{2,1,0:T(8,128)S(1)}) custom-call(f32[4864,128]{1,0:T(8,128)S(1)} %bitcast.9, f32[4,64,256]{2,1,0:T(8,128)S(1)} %pad_maximum_fusion.state), custom_call_target="tpu_custom_call" | custom-call | tf_op jit(solution)/shard_map/sum_rows/pallas_call | solution.py:253
  54.4 0.2 collective-permute-start.2
  54.6 2.7 %collective-permute-start.3 = (f32[4,8,128]{2,1,0:T(8,128)S(1)}, f32[4,8,128]{2,1,0:T(8,128)S(1)}, u32[]{:S(2)}, u32[]{:S(2)}) collective-permute-start(f32[4,8,128]{2,1,0:T(8,128)S(1)} %get-tuple-element.13), channel_id=1, source_target_pairs={{0,1},{1,0},{2,3},{3,2},{4,8},{5,9},{6,10},{7,11},{8,4},{9,5},{10,... | collective-permute-start | bytes 49160 | tf_op jit(solution)/shard_map/ppermute | solution.py:390
  57.3 0.0 collective-permute-done.5.state_beside
  57.3 0.0 collective-permute-done.4.state_pair
  57.3 0.0 collective-permute-done.2.pair
  57.3 2.6 %collective-permute-done.3.beside = f32[4,8,128]{2,1,0:T(8,128)S(1)} collective-permute-done((f32[4,8,128]{2,1,0:T(8,128)S(1)}, f32[4,8,128]{2,1,0:T(8,128)S(1)}, u32[]{:S(2)}, u32[]{:S(2)}) %collective-permute-start.3) | collective-permute-done | bytes 16416 | tf_op jit(solution)/shard_map/ppermute | solution.py:390
  59.9 1.3 %substeps.1 = (f32[4,64,128]{2,1,0:T(8,128)}, f32[64,128]{1,0:T(8,128)}, f32[64,128]{1,0:T(8,128)}, f32[64,128]{1,0:T(8,128)}) custom-call(f32[4,64,256]{2,1,0:T(8,128)S(1)} %pad_maximum_fusion.state, f32[4,64,128]{2,1,0:T(8,128)S(1)} %get-tuple-element.10.flux, f32[3,64,256]{2,1,0:T(8,128)S(1)} %get-tuple-element.11.wide, ...), custom_call_target="tpu_custom_call" | custom-call | tf_op jit(solution)/shard_map/substeps/pallas_call | solution.py:360
  (5 shorter events, 0.0 us)
Async XLA Ops:
  9.3 10.6 %copy-start = (f32[64,128]{1,0:T(8,128)S(1)}, f32[64,128]{1,0:T(8,128)}, u32[]{:S(2)}) copy-start(f32[64,128]{1,0:T(8,128)} %param.17) | copy-start | bytes 98308
  9.3 10.6 %copy-start.1 = (f32[64,128]{1,0:T(8,128)S(1)}, f32[64,128]{1,0:T(8,128)}, u32[]{:S(2)}) copy-start(f32[64,128]{1,0:T(8,128)} %param.16) | copy-start | bytes 98308
  9.3 10.6 %copy-start.2 = (f32[64,128]{1,0:T(8,128)S(1)}, f32[64,128]{1,0:T(8,128)}, u32[]{:S(2)}) copy-start(f32[64,128]{1,0:T(8,128)} %param.15) | copy-start | bytes 98308
  9.3 10.6 %copy-start.3 = (f32[64,128]{1,0:T(8,128)S(1)}, f32[64,128]{1,0:T(8,128)}, u32[]{:S(2)}) copy-start(f32[64,128]{1,0:T(8,128)} %param.14) | copy-start | bytes 98308
  9.3 44.0 %all-to-all-start = ((f32[4864,1,128]{2,1,0:T(1,128)}), f32[4864,1,128]{2,1,0:T(1,128)S(1)}, u32[]{:S(2)}, u32[]{:S(2)}) async-start(f32[4864,1,128]{2,1,0:T(1,128)} %bitcast.10), calls=%async_computation | async-start | bytes 4980736 | tf_op jit(solution)/shard_map/all_to_all | solution.py:409
  20.0 31.5 %collective-permute-start = (f32[4,64,6]{2,1,0:T(8,128)S(1)}, f32[4,64,6]{2,1,0:T(8,128)S(1)}, u32[]{:S(2)}, u32[]{:S(2)}) collective-permute-start(f32[4,64,6]{2,1,0:T(8,128)S(1)} %get-tuple-element.16), channel_id=1, source_target_pairs={{0,3},{1,0},{2,1},{3,2},{4,7},{5,4},{6,5},{7,6},{8,11},{9,8},{10,9... | collective-permute-start | bytes 18440 | tf_op jit(solution)/shard_map/ppermute | solution.py:373
  23.5 33.8 %collective-permute-start.5 = (f32[4,8,128]{2,1,0:T(8,128)S(1)}, f32[4,8,128]{2,1,0:T(8,128)S(1)}, u32[]{:S(2)}, u32[]{:S(2)}) collective-permute-start(f32[4,8,128]{2,1,0:T(8,128)S(1)} %get-tuple-element.14), channel_id=1, source_target_pairs={{0,1},{1,0},{2,3},{3,2},{4,8},{5,9},{6,10},{7,11},{8,4},{9,5},{10,... | collective-permute-start | bytes 49160 | tf_op jit(solution)/shard_map/ppermute | solution.py:390
  25.8 31.5 %collective-permute-start.4 = (f32[4,8,128]{2,1,0:T(8,128)S(1)}, f32[4,8,128]{2,1,0:T(8,128)S(1)}, u32[]{:S(2)}, u32[]{:S(2)}) collective-permute-start(f32[4,8,128]{2,1,0:T(8,128)S(1)} %get-tuple-element.15), channel_id=1, source_target_pairs={{0,4},{4,0},{8,12},{12,8},{16,20},{20,16},{24,28},{28,24},{32,36},... | collective-permute-start | bytes 49160 | tf_op jit(solution)/shard_map/ppermute | solution.py:377
  25.8 27.4 %collective-permute-start.1 = (f32[4,64,6]{2,1,0:T(8,128)S(1)}, f32[4,64,6]{2,1,0:T(8,128)S(1)}, u32[]{:S(2)}, u32[]{:S(2)}) collective-permute-start(f32[4,64,6]{2,1,0:T(8,128)S(1)} %get-tuple-element.17), channel_id=1, source_target_pairs={{0,1},{1,2},{2,3},{3,0},{4,5},{5,6},{6,7},{7,4},{8,9},{9,10},{10,1... | collective-permute-start | bytes 18440 | tf_op jit(solution)/shard_map/ppermute | solution.py:373
  54.4 2.9 %collective-permute-start.2 = (f32[4,8,128]{2,1,0:T(8,128)S(1)}, f32[4,8,128]{2,1,0:T(8,128)S(1)}, u32[]{:S(2)}, u32[]{:S(2)}) collective-permute-start(f32[4,8,128]{2,1,0:T(8,128)S(1)} %get-tuple-element.12), channel_id=1, source_target_pairs={{0,4},{4,0},{8,12},{12,8},{16,20},{20,16},{24,28},{28,24},{32,36},... | collective-permute-start | bytes 49160 | tf_op jit(solution)/shard_map/ppermute | solution.py:377
  54.6 5.3 %collective-permute-start.3 = (f32[4,8,128]{2,1,0:T(8,128)S(1)}, f32[4,8,128]{2,1,0:T(8,128)S(1)}, u32[]{:S(2)}, u32[]{:S(2)}) collective-permute-start(f32[4,8,128]{2,1,0:T(8,128)S(1)} %get-tuple-element.13), channel_id=1, source_target_pairs={{0,1},{1,0},{2,3},{3,2},{4,8},{5,9},{6,10},{7,11},{8,4},{9,5},{10,... | collective-permute-start | bytes 49160 | tf_op jit(solution)/shard_map/ppermute | solution.py:390

commit v5 on v4

--- a/solution.py
+++ b/solution.py
@@ -1,11 +1,12 @@
 import functools
+import math
 
 import jax
 import jax.numpy as jnp
 from jax import lax
 from jax.experimental import pallas as pl
 from jax.experimental.pallas import tpu as pltpu
-from jax.sharding import PartitionSpec as P
+from jax.sharding import Mesh, PartitionSpec as P
 
 CX = 64
 STEPS = 3
@@ -19,7 +20,6 @@
 SPLIT = 5
 LABELS = 96
 CHUNKS = 24
-GROUP = 4
 
 courant = 0.5
 forcing = 0.3
@@ -27,7 +27,10 @@
 damping = 0.05
 steric = 0.5
 
-AXES = ("atm", "ocn")
+SIZES = (4, 4, 2, 4)
+AXES = ("x", "y", "core", "ocn")
+ATM = AXES[:3]
+PEERS = ("core", "ocn", "y", "x")
 
 
 def pack_kernel(
@@ -39,18 +42,19 @@
     out,
     weights,
     lhs,
-    labels,
     src,
     owner,
     target,
     block,
-    count,
+    row_of,
+    first_row,
     built,
     sems,
     small_sems,
     out_sems,
     *,
-    devices,
+    order,
+    stride,
     ocn,
 ):
     total = weights.shape[0]
@@ -71,14 +75,13 @@
     ]
     for copy in copies:
         copy.start(priority=1)
+    devices = len(order)
+    lane = lax.broadcasted_iota(jnp.int32, (devices, B), 1)
     built[...] = jnp.zeros(built.shape, jnp.float32)
-    labels[...] = jnp.full(labels.shape, -1.0, jnp.float32)
-
-    def clear(i, carry):
-        count[i] = 0
-        return carry
-
-    lax.fori_loop(0, devices, clear, 0, unroll=8)
+    built[pl.ds(37, devices, stride=ROWS), :] = jnp.where(lane < LABELS, 0.0, -1.0)
+    for o, at in enumerate(order):
+        row_of[o] = at * ROWS
+        first_row[o] = at * ROWS
     smalls[0].wait()
     zero = jnp.zeros((F, B), jnp.float32)
     for b in range(src.shape[1] // B):
@@ -89,7 +92,7 @@
             lhs[j, b] = jnp.concatenate(parts, 0).astype(jnp.bfloat16)
     for copy in smalls[1:]:
         copy.wait()
-    lane = lax.broadcasted_iota(jnp.int32, (1, B), 1)
+    slot = F * (lax.broadcasted_iota(jnp.int32, (1, B), 1) - LABELS)
     for c in range(CHUNKS):
         copies[c].wait()
         for w in range(c * per, (c + 1) * per, 4):
@@ -98,15 +101,16 @@
             rows = jnp.dot(left, right, preferred_element_type=jnp.float32)
             for j in range(4):
                 o = owner[0, w + j]
-                k = count[o]
-                count[o] = k + 1
-                built[pl.ds(o * ROWS + k * F, F), :] = rows[F * j : F * (j + 1)]
+                row = row_of[o]
+                first = first_row[o]
+                row_of[o] = row + F
+                built[pl.ds(row, F), :] = rows[F * j : F * (j + 1)]
                 name = jnp.full((1, B), target[w + j].astype(jnp.float32))
-                pltpu.store(labels.at[pl.ds(o, 1), :], name, mask=lane == k)
-
-    group = GROUP * ocn
+                pltpu.store(built.at[pl.ds(first + 37, 1), :], name, mask=slot == row - first)
+
+    group = stride * ocn
     lane = lax.broadcasted_iota(jnp.int32, (group, B), 1)
-    place = lax.broadcasted_iota(jnp.int32, (group, B), 0) % ocn
+    place = lax.broadcasted_iota(jnp.int32, (group, B), 0) // stride
     sends = []
     for g in range(devices // group):
         base = g * group * ROWS
@@ -122,17 +126,16 @@
                 edge[part] = jnp.where((lane >= at) & (lane < at + 2 * width), moved, edge[part])
                 from_before[part] |= (lane >= at) & (lane < at + width)
         sides = [
-            jnp.where(mask, pltpu.roll(value, 1, 0), pltpu.roll(value, group - 1, 0))
+            jnp.where(mask, pltpu.roll(value, stride, 0), pltpu.roll(value, group - stride, 0))
             for mask, value in zip(from_before, edge)
         ]
-        own = labels[pl.ds(g * group, group), :]
-        before = jnp.where(place > 0, pltpu.roll(own, 1, 0), -1.0)
-        after = jnp.where(place < ocn - 1, pltpu.roll(own, group - 1, 0), -1.0)
+        own = built[pl.ds(base + 37, group, stride=ROWS), :]
+        before = jnp.where(place > 0, pltpu.roll(own, stride, 0), -1.0)
+        after = jnp.where(place < ocn - 1, pltpu.roll(own, group - stride, 0), -1.0)
         for i, names in enumerate((own, before, after)):
             at = LABELS + CAP * i
-            sides[1] = jnp.where(
-                (lane >= at) & (lane < at + CAP), pltpu.roll(names, at, 1), sides[1]
-            )
+            names = pltpu.roll(names, CAP * i, 1) if i else names
+            sides[1] = jnp.where((lane >= at) & (lane < at + CAP), names, sides[1])
         built[pl.ds(base + 36, group, stride=ROWS), :] = sides[0]
         built[pl.ds(base + 37, group, stride=ROWS), :] = sides[1]
         span = pl.ds(base, group * ROWS)
@@ -143,27 +146,37 @@
         send.wait()
 
 
-def pack(owner, target, block, src, weights, devices, ocn):
+def pack(owner, target, block, src, weights):
     total = weights.shape[0]
+    sizes = [lax.axis_size(axis) for axis in AXES]
+    devices = math.prod(sizes)
+    order = []
+    for o in range(devices):
+        at = 0
+        for axis in PEERS:
+            i = AXES.index(axis)
+            at = at * sizes[i] + o // math.prod(sizes[i + 1 :]) % sizes[i]
+        order.append(at)
+    stride, ocn = sizes[0] * sizes[1], sizes[3]
     here = pl.BlockSpec(memory_space=pltpu.HBM)
     return pl.pallas_call(
-        functools.partial(pack_kernel, devices=devices, ocn=ocn),
+        functools.partial(pack_kernel, order=tuple(order), stride=stride, ocn=ocn),
         out_shape=jax.ShapeDtypeStruct((devices * ROWS, B), jnp.float32),
         in_specs=[here] * 5,
         out_specs=here,
         scratch_shapes=[
             pltpu.VMEM(weights.shape, jnp.bfloat16),
             pltpu.VMEM((4, src.shape[1] // B, 4 * F, B), jnp.bfloat16),
-            pltpu.VMEM((devices, B), jnp.float32),
             pltpu.VMEM(src.shape, jnp.bfloat16),
             pltpu.SMEM((1, total), jnp.int32),
             pltpu.SMEM((total,), jnp.int32),
             pltpu.SMEM((total,), jnp.int32),
             pltpu.SMEM((devices,), jnp.int32),
+            pltpu.SMEM((devices,), jnp.int32),
             pltpu.VMEM((devices * ROWS, B), jnp.float32),
             pltpu.SemaphoreType.DMA((CHUNKS,)),
             pltpu.SemaphoreType.DMA((4,)),
-            pltpu.SemaphoreType.DMA((devices // (GROUP * ocn),)),
+            pltpu.SemaphoreType.DMA((devices // (stride * ocn),)),
         ],
         compiler_params=pltpu.CompilerParams(vmem_limit_bytes=60 << 20),
         cost_estimate=pl.CostEstimate(
@@ -234,7 +247,7 @@
         fields.append(jnp.concatenate([value, outer], axis=1))
     for i, field in enumerate(fields):
         wide[i] = field
-    odd = lax.axis_index("atm") % 2 == 1
+    odd = lax.axis_index("core") == 1
     outers = [field[:, B:] for field in fields] + [state[i, :, B:] for i in range(4)]
     top, bottom = slice(0, 8), slice(CX - 8, CX)
     for rows, other, message in ((top, bottom, to_pair), (bottom, top, to_beside)):
@@ -284,8 +297,9 @@
     send = pltpu.make_async_copy(flux, flux_out, sem)
     send.start()
     rows = CX + 16
-    line = lax.axis_index("atm")
-    odd = line % 2 == 1
+    core = lax.axis_index("core")
+    line = (lax.axis_index("x") * lax.axis_size("y") + lax.axis_index("y")) * 2 + core
+    odd = core == 1
     has_above = line > 0
     has_below = line < lines - 1
 
@@ -373,12 +387,20 @@
     return lax.ppermute(x, axis, [(i, (i + by) % n) for i in range(n)])
 
 
+def packed(x):
+    return x.transpose(0, 2, 1).reshape(-1, B)
+
+
+def unpacked(x):
+    return x.reshape(4, REACH, CX).transpose(0, 2, 1)
+
+
 def with_pair(x):
-    return lax.ppermute(x, "atm", [(i, i ^ 1) for i in range(lax.axis_size("atm"))])
+    return lax.ppermute(x, ATM, [(i, i ^ 1) for i in range(lax.axis_size(ATM))])
 
 
 def with_beside(x):
-    lines, columns = lax.axis_size("atm"), lax.axis_size("ocn")
+    lines, columns = lax.axis_size(ATM), lax.axis_size("ocn")
     partners = []
     for i in range(lines):
         other = i + 1 if i % 2 else i - 1
@@ -402,24 +424,24 @@
     ocean_depth,
 ):
     ocn = lax.axis_size("ocn")
-    devices = lax.axis_size("atm") * ocn
+    lines = lax.axis_size(ATM)
+    devices = lines * ocn
     messages = pack(
-        owner_device.T, target_row, source_block, source_flux, remap_weights, devices, ocn
+        owner_device.T, target_row, source_block, source_flux, remap_weights
     )
     arrived = lax.all_to_all(
-        messages.reshape(-1, 1, B), AXES, split_axis=0, concat_axis=0, tiled=True
+        messages.reshape(-1, 1, B), PEERS, split_axis=0, concat_axis=0, tiled=True
     ).reshape(-1, B)
 
     column = lax.axis_index("ocn")
-    lines = lax.axis_size("atm")
     state = jnp.stack([sea_height, u_velocity, v_velocity, ocean_depth])
     state, messages = lax.optimization_barrier((state, messages))
-    odd = lax.axis_index("atm") % 2 == 1
+    odd = lax.axis_index("core") == 1
     firsts, lasts = state[:, :8], state[:, CX - 8 :]
     state_pair = with_pair(jnp.where(odd, firsts, lasts))
     state_beside = with_beside(jnp.where(odd, lasts, firsts))
-    before = around(state[:, :, B - REACH :], "ocn", 1)
-    after = around(state[:, :, :REACH], "ocn", -1)
+    before = unpacked(around(packed(state[:, :, B - REACH :]), "ocn", 1))
+    after = unpacked(around(packed(state[:, :, :REACH]), "ocn", -1))
     before = jnp.where(column > 0, before, 0.0)
     after = jnp.where(column < ocn - 1, after, 0.0)
     gap = jnp.zeros((4, CX, B - 2 * REACH), jnp.float32)
@@ -432,21 +454,23 @@
 
 
 def solution(mesh):
+    mesh = Mesh(mesh.devices.reshape(SIZES), AXES)
+    cells = P(ATM, "ocn")
     placed = (
         P(None, AXES),
         P(AXES, None, None),
         P(AXES),
         P(AXES, None),
         P(AXES),
-        P("atm", "ocn"),
-        P("atm", "ocn"),
-        P("atm", "ocn"),
-        P("atm", "ocn"),
+        cells,
+        cells,
+        cells,
+        cells,
     )
     return jax.shard_map(
         on_device,
         mesh=mesh,
         in_specs=placed,
-        out_specs=(P(None, "atm", "ocn"), P("atm", "ocn"), P("atm", "ocn"), P("atm", "ocn")),
+        out_specs=(P(None, ATM, "ocn"), cells, cells, cells),
         check_vma=False,
     )

time: 62.4 us -> 61.2 us (0.981); the launches traced: 61.2 us -> 61 us
  starting transfers between devices: 19.1 us -> 17.7 us
  local copies, waits for them, and re-layouts: 0.19 us -> 0.91 us
    ppermute x2, waiting for transfers between devices: 27.3 us -> 12.6 us  [around(): return lax.ppermute(x, axis, [(i, (i + by) % n) for i in range(n)])]
    all_to_all x1, waiting for transfers between devices: 0.01 us -> 13.4 us  [on_device(): lax.all_to_all(messages.reshape(-1, 1, B), PEERS, split_axis=0, concat_ax...]
    ppermute x2, starting transfers between devices: 5 us -> 3.36 us  [with_beside(): return lax.ppermute(x, AXES, partners)]
    ppermute x2, waiting for transfers between devices: 2.6 us -> 4.18 us  [with_beside(): return lax.ppermute(x, AXES, partners)]
  transfers between devices with their start and end apart: 7 -> 7, of which waited for: 3 -> 4; matrix products, arithmetic and copies ran while one was open for 1% -> 2% of each run, Pallas kernels for 2% -> 2%
where the time goes in v5:
time: 61.2 us; the launch traced here: 61 us
  waiting for transfers between devices  30.4 us (50%)
  starting transfers between devices  17.7 us (29%)
  Pallas kernels  11.1 us (18%)
  local copies, waits for them, and re-layouts  0.91 us (1%)
  between operations  0.77 us (1%)
    all_to_all x1, waiting for transfers between devices, on_device(): lax.all_to_all(messages.reshape(-1, 1, B), PEERS, split_axis=0, concat_ax...  13.4 us
    ppermute x2, waiting for transfers between devices, around(): return lax.ppermute(x, axis, [(i, (i + by) % n) for i in range(n)])  12.6 us
    all_to_all x1, starting transfers between devices, on_device(): lax.all_to_all(messages.reshape(-1, 1, B), PEERS, split_axis=0, concat_ax...  10.5 us
    pallas_call x1, Pallas kernels, pack(): pl.pallas_call(functools.partial(pack_kernel, order=tuple(order), stride=...  8.7 us
    ppermute x2, waiting for transfers between devices, with_beside(): return lax.ppermute(x, AXES, partners)  4.18 us
    ppermute x2, starting transfers between devices, around(): return lax.ppermute(x, axis, [(i, (i + by) % n) for i in range(n)])  3.78 us
    ppermute x2, starting transfers between devices, with_beside(): return lax.ppermute(x, AXES, partners)  3.36 us
    pallas_call x1, Pallas kernels, substeps(): pl.pallas_call(functools.partial(step_kernel, lines=lines), out_shape=(ja...  1.31 us
  transfers between devices with their start and end apart: 7, of which 4 were waited for; matrix products, arithmetic and copies ran while one was open for 2% of the time, Pallas kernels for 2%

profile of v5, /device:TPU:4, one launch (start us, length us, event | category | flops | bytes accessed | tf_op | source)
XLA Modules:
  0.0 61.0 jit_solution(10634197099955390867)
XLA Ops:
  0.6 8.7 %remap_pack.1 = f32[4864,128]{1,0:T(8,128)} custom-call(s32[1,576]{1,0:T(1,128)} %bitcast.23, s32[576]{0:T(1024)} %target_h.1, s32[576]{0:T(1024)} %block_h.1, bf16[4,2048]{1,0:T(4,128)(2,1)} %src_h.1, bf16[576,128,128]{2,1,0:T(8,128)(2,1)} %weights_h.1), custom_call_target="tpu_custom_call" | custom-call | flops 75497472 | bytes 18874368 | tf_op jit(solution)/shard_map/remap_pack/pallas_call | solution.py:162
  9.3 0.0 copy-start
  9.4 0.0 copy-start.1
  9.4 0.0 copy-start.2
  9.4 0.0 copy-start.3
  9.4 10.5 %all-to-all-start = ((f32[4864,1,128]{2,1,0:T(1,128)}), f32[4864,1,128]{2,1,0:T(1,128)S(1)}, u32[]{:S(2)}, u32[]{:S(2)}) async-start(f32[4864,1,128]{2,1,0:T(1,128)} %bitcast.16), calls=%async_computation | async-start | bytes 4980736 | tf_op jit(solution)/shard_map/all_to_all | solution.py:432
  19.9 0.0 copy-done
  19.9 0.0 copy-done.1
  19.9 0.0 copy-done.2
  19.9 0.0 copy-done.3
  20.0 0.1 slice_bitcast_fusion.1
  20.1 0.1 copy.19
  20.2 0.1 reshape.29
  20.2 1.6 %collective-permute-start.1 = (f32[12,128]{1,0:T(8,128)S(1)}, f32[12,128]{1,0:T(8,128)S(1)}, u32[]{:S(2)}, u32[]{:S(2)}) collective-permute-start(f32[12,128]{1,0:T(8,128)S(1)} %reshape.29), channel_id=1, source_target_pairs={{0,1},{1,2},{2,3},{3,0},{4,5},{5,6},{6,7},{7,4},{8,9},{9,10},{10,1... | collective-permute-start | bytes 18440 | tf_op jit(solution)/shard_map/ppermute | solution.py:387
  21.9 2.3 %collective-permute-start.5 = (f32[4,8,128]{2,1,0:T(8,128)S(1)}, f32[4,8,128]{2,1,0:T(8,128)S(1)}, u32[]{:S(2)}, u32[]{:S(2)}) collective-permute-start(f32[4,8,128]{2,1,0:T(8,128)S(1)} %get-tuple-element.14), channel_id=1, source_target_pairs={{0,1},{1,0},{2,3},{3,2},{4,8},{5,9},{6,10},{7,11},{8,4},{9,5},{10,... | collective-permute-start | bytes 49160 | tf_op jit(solution)/shard_map/ppermute | solution.py:412
  24.2 0.0 collective-permute-start.4
  24.2 0.1 copy.17
  24.3 0.1 reshape.28
  24.4 2.1 %collective-permute-start = (f32[12,128]{1,0:T(8,128)S(1)}, f32[12,128]{1,0:T(8,128)S(1)}, u32[]{:S(2)}, u32[]{:S(2)}) collective-permute-start(f32[12,128]{1,0:T(8,128)S(1)} %reshape.28), channel_id=1, source_target_pairs={{0,3},{1,0},{2,1},{3,2},{4,7},{5,4},{6,5},{7,6},{8,11},{9,8},{10,9... | collective-permute-start | bytes 18440 | tf_op jit(solution)/shard_map/ppermute | solution.py:387
  26.5 0.1 pad.2.clone
  26.6 12.6 %collective-permute-done.1 = f32[12,128]{1,0:T(8,128)S(1)} collective-permute-done((f32[12,128]{1,0:T(8,128)S(1)}, f32[12,128]{1,0:T(8,128)S(1)}, u32[]{:S(2)}, u32[]{:S(2)}) %collective-permute-start.1) | collective-permute-done | bytes 6176 | tf_op jit(solution)/shard_map/ppermute | solution.py:387
  39.3 0.1 select_n.44
  39.3 0.0 collective-permute-done
  39.3 0.1 select_n.40
  39.4 0.1 copy.18
  39.5 0.1 copy.20
  39.7 0.1 pad_maximum_fusion.state
  39.8 13.4 %all-to-all-done = f32[4864,1,128]{2,1,0:T(1,128)S(1)} async-done(((f32[4864,1,128]{2,1,0:T(1,128)}), f32[4864,1,128]{2,1,0:T(1,128)S(1)}, u32[]{:S(2)}, u32[]{:S(2)}) %all-to-all-start) | async-done | bytes 2490400 | tf_op jit(solution)/shard_map/all_to_all | solution.py:432
  53.2 1.0 %sum_rows.1 = (f32[4,64,128]{2,1,0:T(8,128)S(1)}, f32[3,64,256]{2,1,0:T(8,128)S(1)}, f32[4,8,128]{2,1,0:T(8,128)S(1)}, f32[4,8,128]{2,1,0:T(8,128)S(1)}) custom-call(f32[4864,128]{1,0:T(8,128)S(1)} %bitcast.15, f32[4,64,256]{2,1,0:T(8,128)S(1)} %pad_maximum_fusion.state), custom_call_target="tpu_custom_call" | custom-call | tf_op jit(solution)/shard_map/sum_rows/pallas_call | solution.py:266
  54.2 0.1 collective-permute-start.2
  54.3 1.0 %collective-permute-start.3 = (f32[4,8,128]{2,1,0:T(8,128)S(1)}, f32[4,8,128]{2,1,0:T(8,128)S(1)}, u32[]{:S(2)}, u32[]{:S(2)}) collective-permute-start(f32[4,8,128]{2,1,0:T(8,128)S(1)} %get-tuple-element.13), channel_id=1, source_target_pairs={{0,1},{1,0},{2,3},{3,2},{4,8},{5,9},{6,10},{7,11},{8,4},{9,5},{10,... | collective-permute-start | bytes 49160 | tf_op jit(solution)/shard_map/ppermute | solution.py:412
  55.4 0.0 collective-permute-done.5.state_beside
  55.4 0.0 collective-permute-done.4.state_pair
  55.4 0.1 collective-permute-done.2.pair
  55.5 4.2 %collective-permute-done.3.beside = f32[4,8,128]{2,1,0:T(8,128)S(1)} collective-permute-done((f32[4,8,128]{2,1,0:T(8,128)S(1)}, f32[4,8,128]{2,1,0:T(8,128)S(1)}, u32[]{:S(2)}, u32[]{:S(2)}) %collective-permute-start.3) | collective-permute-done | bytes 16416 | tf_op jit(solution)/shard_map/ppermute | solution.py:412
  59.7 1.3 %substeps.1 = (f32[4,64,128]{2,1,0:T(8,128)}, f32[64,128]{1,0:T(8,128)}, f32[64,128]{1,0:T(8,128)}, f32[64,128]{1,0:T(8,128)}) custom-call(f32[4,64,256]{2,1,0:T(8,128)S(1)} %pad_maximum_fusion.state, f32[4,64,128]{2,1,0:T(8,128)S(1)} %get-tuple-element.10.flux, f32[3,64,256]{2,1,0:T(8,128)S(1)} %get-tuple-element.11.wide, ...), custom_call_target="tpu_custom_call" | custom-call | tf_op jit(solution)/shard_map/substeps/pallas_call | solution.py:374
  (5 shorter events, 0.0 us)
Async XLA Ops:
  9.3 10.6 %copy-start = (f32[64,128]{1,0:T(8,128)S(1)}, f32[64,128]{1,0:T(8,128)}, u32[]{:S(2)}) copy-start(f32[64,128]{1,0:T(8,128)} %param.17) | copy-start | bytes 98308
  9.4 10.6 %copy-start.1 = (f32[64,128]{1,0:T(8,128)S(1)}, f32[64,128]{1,0:T(8,128)}, u32[]{:S(2)}) copy-start(f32[64,128]{1,0:T(8,128)} %param.16) | copy-start | bytes 98308
  9.4 10.6 %copy-start.2 = (f32[64,128]{1,0:T(8,128)S(1)}, f32[64,128]{1,0:T(8,128)}, u32[]{:S(2)}) copy-start(f32[64,128]{1,0:T(8,128)} %param.15) | copy-start | bytes 98308
  9.4 10.6 %copy-start.3 = (f32[64,128]{1,0:T(8,128)S(1)}, f32[64,128]{1,0:T(8,128)}, u32[]{:S(2)}) copy-start(f32[64,128]{1,0:T(8,128)} %param.14) | copy-start | bytes 98308
  9.4 43.8 %all-to-all-start = ((f32[4864,1,128]{2,1,0:T(1,128)}), f32[4864,1,128]{2,1,0:T(1,128)S(1)}, u32[]{:S(2)}, u32[]{:S(2)}) async-start(f32[4864,1,128]{2,1,0:T(1,128)} %bitcast.16), calls=%async_computation | async-start | bytes 4980736 | tf_op jit(solution)/shard_map/all_to_all | solution.py:432
  20.2 19.0 %collective-permute-start.1 = (f32[12,128]{1,0:T(8,128)S(1)}, f32[12,128]{1,0:T(8,128)S(1)}, u32[]{:S(2)}, u32[]{:S(2)}) collective-permute-start(f32[12,128]{1,0:T(8,128)S(1)} %reshape.29), channel_id=1, source_target_pairs={{0,1},{1,2},{2,3},{3,0},{4,5},{5,6},{6,7},{7,4},{8,9},{9,10},{10,1... | collective-permute-start | bytes 18440 | tf_op jit(solution)/shard_map/ppermute | solution.py:387
  21.9 33.5 %collective-permute-start.5 = (f32[4,8,128]{2,1,0:T(8,128)S(1)}, f32[4,8,128]{2,1,0:T(8,128)S(1)}, u32[]{:S(2)}, u32[]{:S(2)}) collective-permute-start(f32[4,8,128]{2,1,0:T(8,128)S(1)} %get-tuple-element.14), channel_id=1, source_target_pairs={{0,1},{1,0},{2,3},{3,2},{4,8},{5,9},{6,10},{7,11},{8,4},{9,5},{10,... | collective-permute-start | bytes 49160 | tf_op jit(solution)/shard_map/ppermute | solution.py:412
  24.2 31.2 %collective-permute-start.4 = (f32[4,8,128]{2,1,0:T(8,128)S(1)}, f32[4,8,128]{2,1,0:T(8,128)S(1)}, u32[]{:S(2)}, u32[]{:S(2)}) collective-permute-start(f32[4,8,128]{2,1,0:T(8,128)S(1)} %get-tuple-element.15), channel_id=1, source_target_pairs={{0,4},{4,0},{8,12},{12,8},{16,20},{20,16},{24,28},{28,24},{32,36},... | collective-permute-start | bytes 49160 | tf_op jit(solution)/shard_map/ppermute | solution.py:399
  24.4 15.0 %collective-permute-start = (f32[12,128]{1,0:T(8,128)S(1)}, f32[12,128]{1,0:T(8,128)S(1)}, u32[]{:S(2)}, u32[]{:S(2)}) collective-permute-start(f32[12,128]{1,0:T(8,128)S(1)} %reshape.28), channel_id=1, source_target_pairs={{0,3},{1,0},{2,1},{3,2},{4,7},{5,4},{6,5},{7,6},{8,11},{9,8},{10,9... | collective-permute-start | bytes 18440 | tf_op jit(solution)/shard_map/ppermute | solution.py:387
  54.2 1.3 %collective-permute-start.2 = (f32[4,8,128]{2,1,0:T(8,128)S(1)}, f32[4,8,128]{2,1,0:T(8,128)S(1)}, u32[]{:S(2)}, u32[]{:S(2)}) collective-permute-start(f32[4,8,128]{2,1,0:T(8,128)S(1)} %get-tuple-element.12), channel_id=1, source_target_pairs={{0,4},{4,0},{8,12},{12,8},{16,20},{20,16},{24,28},{28,24},{32,36},... | collective-permute-start | bytes 49160 | tf_op jit(solution)/shard_map/ppermute | solution.py:399
  54.3 5.4 %collective-permute-start.3 = (f32[4,8,128]{2,1,0:T(8,128)S(1)}, f32[4,8,128]{2,1,0:T(8,128)S(1)}, u32[]{:S(2)}, u32[]{:S(2)}) collective-permute-start(f32[4,8,128]{2,1,0:T(8,128)S(1)} %get-tuple-element.13), channel_id=1, source_target_pairs={{0,1},{1,0},{2,3},{3,2},{4,8},{5,9},{6,10},{7,11},{8,4},{9,5},{10,... | collective-permute-start | bytes 49160 | tf_op jit(solution)/shard_map/ppermute | solution.py:412

commit v6 on v5

--- a/solution.py
+++ b/solution.py
@@ -346,7 +346,7 @@
     def diff_y(a):
         return pltpu.roll(a, 2 * B - 1, 1) - pltpu.roll(a, 1, 1)
 
-    for _ in range(STEPS):
+    for _ in range(STEPS - 1):
         height = height - slope * (diff_x(zonal) + diff_y(merid)) + source
         new_zonal = (
             (1.0 - damping) * zonal
@@ -362,9 +362,21 @@
         )
         zonal = jnp.where(inside, new_zonal, 0.0)
         merid = jnp.where(inside, new_merid, 0.0)
-    height_out[...] = height[8 : 8 + CX, :B]
-    zonal_out[...] = zonal[8 : 8 + CX, :B]
-    merid_out[...] = merid[8 : 8 + CX, :B]
+    height = height - slope * (diff_x(zonal) + diff_y(merid)) + source
+    own = (slice(8, 8 + CX), slice(0, B))
+    height_out[...] = height[own]
+    zonal_out[...] = (
+        (1.0 - damping) * zonal[own]
+        - (0.5 * courant) * diff_x(height[:, :B])[own]
+        + coriolis * merid[own]
+        + zonal_gain[own]
+    )
+    merid_out[...] = (
+        (1.0 - damping) * merid[own]
+        - (0.5 * courant) * diff_y(height[8 : 8 + CX])[:, :B]
+        - coriolis * zonal[own]
+        + merid_gain[own]
+    )
     send.wait()
 
 

time: 61.2 us -> 61.2 us (level)
  no operation moved by 1% of the time
where the time goes in v6:
time: 61.2 us; the launch traced here: 61 us
  waiting for transfers between devices  30.4 us (50%)
  starting transfers between devices  17.7 us (29%)
  Pallas kernels  11 us (18%)
  local copies, waits for them, and re-layouts  0.91 us (1%)
  between operations  0.77 us (1%)
    all_to_all x1, waiting for transfers between devices, on_device(): lax.all_to_all(messages.reshape(-1, 1, B), PEERS, split_axis=0, concat_ax...  13.4 us
    ppermute x2, waiting for transfers between devices, around(): return lax.ppermute(x, axis, [(i, (i + by) % n) for i in range(n)])  12.6 us
    all_to_all x1, starting transfers between devices, on_device(): lax.all_to_all(messages.reshape(-1, 1, B), PEERS, split_axis=0, concat_ax...  10.5 us
    pallas_call x1, Pallas kernels, pack(): pl.pallas_call(functools.partial(pack_kernel, order=tuple(order), stride=...  8.7 us
    ppermute x2, waiting for transfers between devices, with_beside(): return lax.ppermute(x, AXES, partners)  4.18 us
    ppermute x2, starting transfers between devices, around(): return lax.ppermute(x, axis, [(i, (i + by) % n) for i in range(n)])  3.78 us
    ppermute x2, starting transfers between devices, with_beside(): return lax.ppermute(x, AXES, partners)  3.36 us
    pallas_call x1, Pallas kernels, substeps(): pl.pallas_call(functools.partial(step_kernel, lines=lines), out_shape=(ja...  1.31 us
  transfers between devices with their start and end apart: 7, of which 4 were waited for; matrix products, arithmetic and copies ran while one was open for 2% of the time, Pallas kernels for 2%

profile of v6, /device:TPU:4, one launch (start us, length us, event | category | flops | bytes accessed | tf_op | source)
XLA Modules:
  0.0 61.0 jit_solution(5227550747584278194)
XLA Ops:
  0.6 8.7 %remap_pack.1 = f32[4864,128]{1,0:T(8,128)} custom-call(s32[1,576]{1,0:T(1,128)} %bitcast.23, s32[576]{0:T(1024)} %target_h.1, s32[576]{0:T(1024)} %block_h.1, bf16[4,2048]{1,0:T(4,128)(2,1)} %src_h.1, bf16[576,128,128]{2,1,0:T(8,128)(2,1)} %weights_h.1), custom_call_target="tpu_custom_call" | custom-call | flops 75497472 | bytes 18874368 | tf_op jit(solution)/shard_map/remap_pack/pallas_call | solution.py:162
  9.3 0.0 copy-start
  9.4 0.0 copy-start.1
  9.4 0.0 copy-start.2
  9.4 0.0 copy-start.3
  9.4 10.5 %all-to-all-start = ((f32[4864,1,128]{2,1,0:T(1,128)}), f32[4864,1,128]{2,1,0:T(1,128)S(1)}, u32[]{:S(2)}, u32[]{:S(2)}) async-start(f32[4864,1,128]{2,1,0:T(1,128)} %bitcast.16), calls=%async_computation | async-start | bytes 4980736 | tf_op jit(solution)/shard_map/all_to_all | solution.py:444
  19.9 0.0 copy-done
  19.9 0.0 copy-done.1
  19.9 0.0 copy-done.2
  19.9 0.0 copy-done.3
  20.0 0.1 slice_bitcast_fusion.1
  20.1 0.1 copy.19
  20.2 0.1 reshape.29
  20.2 1.6 %collective-permute-start.1 = (f32[12,128]{1,0:T(8,128)S(1)}, f32[12,128]{1,0:T(8,128)S(1)}, u32[]{:S(2)}, u32[]{:S(2)}) collective-permute-start(f32[12,128]{1,0:T(8,128)S(1)} %reshape.29), channel_id=1, source_target_pairs={{0,1},{1,2},{2,3},{3,0},{4,5},{5,6},{6,7},{7,4},{8,9},{9,10},{10,1... | collective-permute-start | bytes 18440 | tf_op jit(solution)/shard_map/ppermute | solution.py:399
  21.9 2.3 %collective-permute-start.5 = (f32[4,8,128]{2,1,0:T(8,128)S(1)}, f32[4,8,128]{2,1,0:T(8,128)S(1)}, u32[]{:S(2)}, u32[]{:S(2)}) collective-permute-start(f32[4,8,128]{2,1,0:T(8,128)S(1)} %get-tuple-element.14), channel_id=1, source_target_pairs={{0,1},{1,0},{2,3},{3,2},{4,8},{5,9},{6,10},{7,11},{8,4},{9,5},{10,... | collective-permute-start | bytes 49160 | tf_op jit(solution)/shard_map/ppermute | solution.py:424
  24.2 0.0 collective-permute-start.4
  24.2 0.1 copy.17
  24.3 0.1 reshape.28
  24.4 2.1 %collective-permute-start = (f32[12,128]{1,0:T(8,128)S(1)}, f32[12,128]{1,0:T(8,128)S(1)}, u32[]{:S(2)}, u32[]{:S(2)}) collective-permute-start(f32[12,128]{1,0:T(8,128)S(1)} %reshape.28), channel_id=1, source_target_pairs={{0,3},{1,0},{2,1},{3,2},{4,7},{5,4},{6,5},{7,6},{8,11},{9,8},{10,9... | collective-permute-start | bytes 18440 | tf_op jit(solution)/shard_map/ppermute | solution.py:399
  26.5 0.1 pad.2.clone
  26.6 12.6 %collective-permute-done.1 = f32[12,128]{1,0:T(8,128)S(1)} collective-permute-done((f32[12,128]{1,0:T(8,128)S(1)}, f32[12,128]{1,0:T(8,128)S(1)}, u32[]{:S(2)}, u32[]{:S(2)}) %collective-permute-start.1) | collective-permute-done | bytes 6176 | tf_op jit(solution)/shard_map/ppermute | solution.py:399
  39.3 0.1 select_n.44
  39.3 0.0 collective-permute-done
  39.3 0.1 select_n.40
  39.4 0.1 copy.18
  39.5 0.1 copy.20
  39.7 0.1 pad_maximum_fusion.state
  39.8 13.4 %all-to-all-done = f32[4864,1,128]{2,1,0:T(1,128)S(1)} async-done(((f32[4864,1,128]{2,1,0:T(1,128)}), f32[4864,1,128]{2,1,0:T(1,128)S(1)}, u32[]{:S(2)}, u32[]{:S(2)}) %all-to-all-start) | async-done | bytes 2490400 | tf_op jit(solution)/shard_map/all_to_all | solution.py:444
  53.2 1.0 %sum_rows.1 = (f32[4,64,128]{2,1,0:T(8,128)S(1)}, f32[3,64,256]{2,1,0:T(8,128)S(1)}, f32[4,8,128]{2,1,0:T(8,128)S(1)}, f32[4,8,128]{2,1,0:T(8,128)S(1)}) custom-call(f32[4864,128]{1,0:T(8,128)S(1)} %bitcast.15, f32[4,64,256]{2,1,0:T(8,128)S(1)} %pad_maximum_fusion.state), custom_call_target="tpu_custom_call" | custom-call | tf_op jit(solution)/shard_map/sum_rows/pallas_call | solution.py:266
  54.2 0.1 collective-permute-start.2
  54.3 1.0 %collective-permute-start.3 = (f32[4,8,128]{2,1,0:T(8,128)S(1)}, f32[4,8,128]{2,1,0:T(8,128)S(1)}, u32[]{:S(2)}, u32[]{:S(2)}) collective-permute-start(f32[4,8,128]{2,1,0:T(8,128)S(1)} %get-tuple-element.13), channel_id=1, source_target_pairs={{0,1},{1,0},{2,3},{3,2},{4,8},{5,9},{6,10},{7,11},{8,4},{9,5},{10,... | collective-permute-start | bytes 49160 | tf_op jit(solution)/shard_map/ppermute | solution.py:424
  55.4 0.0 collective-permute-done.5.state_beside
  55.4 0.0 collective-permute-done.4.state_pair
  55.4 0.1 collective-permute-done.2.pair
  55.5 4.2 %collective-permute-done.3.beside = f32[4,8,128]{2,1,0:T(8,128)S(1)} collective-permute-done((f32[4,8,128]{2,1,0:T(8,128)S(1)}, f32[4,8,128]{2,1,0:T(8,128)S(1)}, u32[]{:S(2)}, u32[]{:S(2)}) %collective-permute-start.3) | collective-permute-done | bytes 16416 | tf_op jit(solution)/shard_map/ppermute | solution.py:424
  59.7 1.3 %substeps.1 = (f32[4,64,128]{2,1,0:T(8,128)}, f32[64,128]{1,0:T(8,128)}, f32[64,128]{1,0:T(8,128)}, f32[64,128]{1,0:T(8,128)}) custom-call(f32[4,64,256]{2,1,0:T(8,128)S(1)} %pad_maximum_fusion.state, f32[4,64,128]{2,1,0:T(8,128)S(1)} %get-tuple-element.10.flux, f32[3,64,256]{2,1,0:T(8,128)S(1)} %get-tuple-element.11.wide, ...), custom_call_target="tpu_custom_call" | custom-call | tf_op jit(solution)/shard_map/substeps/pallas_call | solution.py:386
  (5 shorter events, 0.0 us)
Async XLA Ops:
  9.3 10.6 %copy-start = (f32[64,128]{1,0:T(8,128)S(1)}, f32[64,128]{1,0:T(8,128)}, u32[]{:S(2)}) copy-start(f32[64,128]{1,0:T(8,128)} %param.17) | copy-start | bytes 98308
  9.4 10.6 %copy-start.1 = (f32[64,128]{1,0:T(8,128)S(1)}, f32[64,128]{1,0:T(8,128)}, u32[]{:S(2)}) copy-start(f32[64,128]{1,0:T(8,128)} %param.16) | copy-start | bytes 98308
  9.4 10.6 %copy-start.2 = (f32[64,128]{1,0:T(8,128)S(1)}, f32[64,128]{1,0:T(8,128)}, u32[]{:S(2)}) copy-start(f32[64,128]{1,0:T(8,128)} %param.15) | copy-start | bytes 98308
  9.4 10.6 %copy-start.3 = (f32[64,128]{1,0:T(8,128)S(1)}, f32[64,128]{1,0:T(8,128)}, u32[]{:S(2)}) copy-start(f32[64,128]{1,0:T(8,128)} %param.14) | copy-start | bytes 98308
  9.4 43.8 %all-to-all-start = ((f32[4864,1,128]{2,1,0:T(1,128)}), f32[4864,1,128]{2,1,0:T(1,128)S(1)}, u32[]{:S(2)}, u32[]{:S(2)}) async-start(f32[4864,1,128]{2,1,0:T(1,128)} %bitcast.16), calls=%async_computation | async-start | bytes 4980736 | tf_op jit(solution)/shard_map/all_to_all | solution.py:444
  20.2 19.0 %collective-permute-start.1 = (f32[12,128]{1,0:T(8,128)S(1)}, f32[12,128]{1,0:T(8,128)S(1)}, u32[]{:S(2)}, u32[]{:S(2)}) collective-permute-start(f32[12,128]{1,0:T(8,128)S(1)} %reshape.29), channel_id=1, source_target_pairs={{0,1},{1,2},{2,3},{3,0},{4,5},{5,6},{6,7},{7,4},{8,9},{9,10},{10,1... | collective-permute-start | bytes 18440 | tf_op jit(solution)/shard_map/ppermute | solution.py:399
  21.9 33.5 %collective-permute-start.5 = (f32[4,8,128]{2,1,0:T(8,128)S(1)}, f32[4,8,128]{2,1,0:T(8,128)S(1)}, u32[]{:S(2)}, u32[]{:S(2)}) collective-permute-start(f32[4,8,128]{2,1,0:T(8,128)S(1)} %get-tuple-element.14), channel_id=1, source_target_pairs={{0,1},{1,0},{2,3},{3,2},{4,8},{5,9},{6,10},{7,11},{8,4},{9,5},{10,... | collective-permute-start | bytes 49160 | tf_op jit(solution)/shard_map/ppermute | solution.py:424
  24.2 31.2 %collective-permute-start.4 = (f32[4,8,128]{2,1,0:T(8,128)S(1)}, f32[4,8,128]{2,1,0:T(8,128)S(1)}, u32[]{:S(2)}, u32[]{:S(2)}) collective-permute-start(f32[4,8,128]{2,1,0:T(8,128)S(1)} %get-tuple-element.15), channel_id=1, source_target_pairs={{0,4},{4,0},{8,12},{12,8},{16,20},{20,16},{24,28},{28,24},{32,36},... | collective-permute-start | bytes 49160 | tf_op jit(solution)/shard_map/ppermute | solution.py:411
  24.4 15.0 %collective-permute-start = (f32[12,128]{1,0:T(8,128)S(1)}, f32[12,128]{1,0:T(8,128)S(1)}, u32[]{:S(2)}, u32[]{:S(2)}) collective-permute-start(f32[12,128]{1,0:T(8,128)S(1)} %reshape.28), channel_id=1, source_target_pairs={{0,3},{1,0},{2,1},{3,2},{4,7},{5,4},{6,5},{7,6},{8,11},{9,8},{10,9... | collective-permute-start | bytes 18440 | tf_op jit(solution)/shard_map/ppermute | solution.py:399
  54.2 1.3 %collective-permute-start.2 = (f32[4,8,128]{2,1,0:T(8,128)S(1)}, f32[4,8,128]{2,1,0:T(8,128)S(1)}, u32[]{:S(2)}, u32[]{:S(2)}) collective-permute-start(f32[4,8,128]{2,1,0:T(8,128)S(1)} %get-tuple-element.12), channel_id=1, source_target_pairs={{0,4},{4,0},{8,12},{12,8},{16,20},{20,16},{24,28},{28,24},{32,36},... | collective-permute-start | bytes 49160 | tf_op jit(solution)/shard_map/ppermute | solution.py:411
  54.3 5.4 %collective-permute-start.3 = (f32[4,8,128]{2,1,0:T(8,128)S(1)}, f32[4,8,128]{2,1,0:T(8,128)S(1)}, u32[]{:S(2)}, u32[]{:S(2)}) collective-permute-start(f32[4,8,128]{2,1,0:T(8,128)S(1)} %get-tuple-element.13), channel_id=1, source_target_pairs={{0,1},{1,0},{2,3},{3,2},{4,8},{5,9},{6,10},{7,11},{8,4},{9,5},{10,... | collective-permute-start | bytes 49160 | tf_op jit(solution)/shard_map/ppermute | solution.py:424
